TPU v7x, 512 devices: a whole 4x4x16 slice. The times are simulated.
512 devices in a mesh: guidance: 2 (over core), context: 16 (over z), head: 16 (over x, y).
Axes of the slice: x: 4, y: 4, z: 16, core: 2. Of those that a mesh axis runs over, the one named last changes fastest.
Arguments:
- tokens: bfloat16 [49152, 3072], P(('guidance', 'context', 'head')), parts along dimension 0, may hold values from -6 to 6
- w_query: bfloat16 [3072, 3072], P('context', 'head'), may hold values from -0.109375 to 0.109375
- w_key: bfloat16 [3072, 3072], P('context', 'head'), may hold values from -0.109375 to 0.109375
- w_value: bfloat16 [3072, 3072], P('context', 'head'), may hold values from -0.109375 to 0.109375
- w_out: bfloat16 [3072, 3072], P('context', 'head'), may hold values from -0.109375 to 0.109375
- q_gain: float32 [64], replicated, may hold values from 0.5 to 8
- k_gain: float32 [64], replicated, may hold values from 0.5 to 8
- key_tiles: int32 [384, 8], P('context'), may hold values from 0 to 383, as said below
- key_count: int32 [384], P('context'), may hold values from 3 to 8, as said below
Outputs:
- projected_out: bfloat16 [49152, 3072], P(('guidance', 'context'), 'head'), parts along dimension 0
There are 2 independent parts, one for each index of `guidance`. A program takes and returns all parts, laid end to end along the dimension named above; an argument that names none is the same for every part. Nothing has to cross between parts.
Inputs may be any that keep to these rules, and one draw needn't show every extreme that they name: `key_tiles`: row q holds 8 different tiles, each in the frame of query tile q or one frame before or after, within one tile row and one tile column of it; the first is tile q itself. `key_count`: the first tile of every frame uses all 8.
All inputs are finite; a program needn't handle non-finite values.
Results may differ from a plain program's by a relative error of at most 0.0075.
The roundings to bfloat16 on the way count: a program that leaves them out, or rounds other values in their place, can miss the bound.
Values may be sent and summed in bfloat16 or wider, within the bound.
A program may use at most 64 MiB of HBM per device.

v0:
```python
import math

import jax
import jax.numpy as jnp
from jax import lax
from jax.sharding import PartitionSpec as P

HEAD_DIM = 64
FRAME_H = 30
FRAME_W = 45
TS = 8
TILES_W = 6
TILES = 24
SLOTS = 1536
KT = 8


def padded(block, sides, width):
    for axis, dim in sides:
        count = lax.axis_size(axis)
        forward = [(i, i + 1) for i in range(count - 1)]
        backward = [(target, source) for source, target in forward]
        low = lax.ppermute(
            lax.slice_in_dim(block, block.shape[dim] - width, None, axis=dim), axis, forward
        )
        high = lax.ppermute(lax.slice_in_dim(block, 0, width, axis=dim), axis, backward)
        block = jnp.concatenate([low, block, high], axis=dim)
    return block


def layer_norm(values, gain):
    mean = jnp.mean(values, axis=-1, keepdims=True)
    centred = values - mean
    spread = jnp.mean(centred * centred, axis=-1, keepdims=True)
    return centred * lax.rsqrt(spread + 1e-06) * gain


def slot_live(tile_ids):
    within = tile_ids % TILES
    slots = jnp.arange(TS * TS, dtype=jnp.int32)
    grid_row = (within // TILES_W)[..., None] * TS + slots // TS
    grid_col = (within % TILES_W)[..., None] * TS + slots % TS
    return (grid_row < FRAME_H) & (grid_col < FRAME_W)


def normed(rows_x, weight, gain):
    raw = jnp.dot(rows_x, weight, preferred_element_type=jnp.float32)
    shaped = raw.reshape(raw.shape[0], -1, HEAD_DIM)
    return layer_norm(shaped, gain).reshape(raw.shape[0], -1).astype(jnp.bfloat16)


def plain(rows_x, weight):
    return jnp.dot(rows_x, weight, preferred_element_type=jnp.float32).astype(jnp.bfloat16)


def block_tokens(tokens):
    return lax.all_gather(tokens, "head", axis=0, tiled=True)


def neighbour_frames(keyval):
    return padded(keyval, (("context", 0),), 1)


def attend(queries, keys, values, keep):
    scale = 1.0 / math.sqrt(HEAD_DIM)
    scores = (
        jnp.einsum("tqhe,tkhe->thqk", queries, keys, preferred_element_type=jnp.float32) * scale
    )
    mask = keep[:, None, None, :]
    scores = jnp.where(mask, scores, -jnp.inf)
    top = jnp.max(scores, axis=-1, keepdims=True)
    expo = jnp.where(mask, jnp.exp(scores - top), 0.0)
    weights = (expo / jnp.sum(expo, axis=-1, keepdims=True)).astype(jnp.bfloat16)
    return jnp.einsum("thqk,tkhe->tqhe", weights, values, preferred_element_type=jnp.float32)


def on_device(tokens, w_query, w_key, w_value, w_out, q_gain, k_gain, key_tiles, key_count):
    width = w_query.shape[1]
    heads_here = width // HEAD_DIM
    area = TS * TS
    query_weight, key_weight, value_weight, out_weight = (
        lax.all_gather(w_query, "context", axis=0, tiled=True),
        lax.all_gather(w_key, "context", axis=0, tiled=True),
        lax.all_gather(w_value, "context", axis=0, tiled=True),
        lax.all_gather(w_out, "context", axis=0, tiled=True),
    )
    whole = block_tokens(tokens)
    frames_here = whole.shape[0] // SLOTS
    projected = jnp.concatenate(
        [
            normed(whole, query_weight, q_gain),
            normed(whole, key_weight, k_gain),
            plain(whole, value_weight),
        ],
        axis=1,
    )
    query = projected[:, :width]
    keyval = projected[:, width:].reshape(frames_here, SLOTS, 2 * width)
    window = neighbour_frames(keyval)
    tiles_here = frames_here * TILES
    window_tiles = window.reshape((frames_here + 2) * TILES, area, 2 * width)
    query_tiles = query.reshape(tiles_here, area, heads_here, HEAD_DIM)
    first_tile = (lax.axis_index("context") * frames_here - 1) * TILES
    local_lists = key_tiles - first_tile
    in_use = jnp.arange(KT, dtype=jnp.int32)[None, :] < key_count[:, None]
    block = math.gcd(tiles_here, 8)

    def attend_block(index):
        start = index * block
        lists = lax.dynamic_slice_in_dim(local_lists, start, block, 0)
        global_lists = lax.dynamic_slice_in_dim(key_tiles, start, block, 0)
        used = lax.dynamic_slice_in_dim(in_use, start, block, 0)
        queries = lax.dynamic_slice_in_dim(query_tiles, start, block, 0)
        gathered = window_tiles[lists]
        keys = gathered[..., :width].reshape(block, KT * area, heads_here, HEAD_DIM)
        values = gathered[..., width:].reshape(block, KT * area, heads_here, HEAD_DIM)
        keep = (used[:, :, None] & slot_live(global_lists)).reshape(block, KT * area)
        result = attend(queries, keys, values, keep)
        own = slot_live(start + jnp.arange(block, dtype=jnp.int32))
        return jnp.where(own[:, :, None, None], result, 0.0).astype(jnp.bfloat16)

    blocks = lax.map(attend_block, jnp.arange(tiles_here // block, dtype=jnp.int32))
    outputs = blocks.reshape(frames_here * SLOTS, width)
    all_heads = lax.all_gather(outputs, "head", axis=1, tiled=True)
    summed = jnp.dot(all_heads, out_weight, preferred_element_type=jnp.float32)
    return summed.astype(jnp.bfloat16)


def solution(mesh):
    in_specs = (
        P(("guidance", "context", "head"), None),
        P("context", "head"),
        P("context", "head"),
        P("context", "head"),
        P("context", "head"),
        P(),
        P(),
        P("context", None),
        P("context"),
    )
    out_specs = P(("guidance", "context"), "head")
    return jax.shard_map(
        on_device, mesh=mesh, in_specs=in_specs, out_specs=out_specs, check_vma=False
    )
```

profile of v0, /device:TPU:1, one launch (start us, length us, event | category | flops | bytes accessed | tf_op | source)
XLA Modules:
  0.0 534.2 jit_solution(7840644386910256759)
XLA Ops:
  13.5 63.8 %all-gather.9.cloned.1.call-done = bf16[3072,192]{1,0:T(8,128)(2,1)} async-done(((bf16[192,192]{1,0:T(8,128)(2,1)}), bf16[3072,192]{1,0:T(8,128)(2,1)}) %all-gather.9.cloned.1.call-update) | async-done | bytes 1179664 | tf_op jit(solution)/shard_map/all_gather | solution.py:83
  77.4 100.8 %all-gather.7.cloned.1.call-done = bf16[1536,3072]{1,0:T(8,128)(2,1)} async-done(((bf16[96,3072]{1,0:T(8,128)(2,1)}), bf16[1536,3072]{1,0:T(8,128)(2,1)}) %all-gather.7.cloned.1.call-update) | async-done | bytes 9437200 | tf_op jit(solution)/shard_map/all_gather | solution.py:57
  178.2 7.3 %fusion.27 = f32[1536,192]{0,1:T(8,128)S(1)} fusion(bf16[1536,3072]{1,0:T(8,128)(2,1)} %all-gather.7.cloned.1.call-done, bf16[3072,192]{1,0:T(8,128)(2,1)} %all-gather.9.cloned.1.call-done), kind=kOutput, calls=%fused_computation.70 | convolution fusion | flops 1811939328 | bytes 11796480 | tf_op jit(solution)/shard_map/dot_general | solution.py:47
  185.9 56.7 %all-gather.11.cloned.1.call-done = bf16[3072,192]{1,0:T(8,128)(2,1)} async-done(((bf16[192,192]{1,0:T(8,128)(2,1)}), bf16[3072,192]{1,0:T(8,128)(2,1)}) %all-gather.11.cloned.1.call-update) | async-done | bytes 1179664 | tf_op jit(solution)/shard_map/all_gather | solution.py:84
  242.7 7.4 %convolution_convert_fusion.1 = bf16[1536,192]{0,1:T(8,128)(2,1)S(1)} fusion(bf16[1536,3072]{1,0:T(8,128)(2,1)} %all-gather.7.cloned.1.call-done, bf16[3072,192]{1,0:T(8,128)(2,1)} %all-gather.11.cloned.1.call-done), kind=kOutput, calls=%fused_computation.50 | convolution fusion | flops 1812234240 | bytes 11206656 | tf_op jit(solution)/shard_map/dot_general | solution.py:53
  251.4 5.0 collective-permute-start
  256.5 59.5 %all-gather.13.cloned.1.call-done = bf16[3072,192]{1,0:T(8,128)(2,1)} async-done(((bf16[192,192]{1,0:T(8,128)(2,1)}), bf16[3072,192]{1,0:T(8,128)(2,1)}) %all-gather.13.cloned.1.call-update) | async-done | bytes 1179664 | tf_op jit(solution)/shard_map/all_gather | solution.py:82
  316.0 7.3 %fusion.28 = f32[1536,192]{0,1:T(8,128)S(1)} fusion(bf16[1536,3072]{1,0:T(8,128)(2,1)} %all-gather.7.cloned.1.call-done, bf16[3072,192]{1,0:T(8,128)(2,1)} %all-gather.13.cloned.1.call-done), kind=kOutput, calls=%fused_computation.71 | convolution fusion | flops 1811939328 | bytes 11796480 | tf_op jit(solution)/shard_map/dot_general | solution.py:47
  327.8 3.7 copy.18
  331.5 90.1 %while.13 = (s32[]{:T(128)}, bf16[3,8,64,3,64]{2,1,0,4,3:T(8,128)(2,1)}, s32[3]{0:T(128)S(1)}, s32[24,8]{1,0:T(8,128)}, bf16[72,64,384]{2,1,0:T(8,128)(2,1)}, /*...) while((s32[]{:T(128)}, ...), condition=%wide.region_7.8_spmd, body=%wide.region_4.7_spmd.sunk | while | flops 208632176 | bytes 48776748 | solution.py:122
  336.6 3.2 gather_fusion
  339.9 3.2 fusion.54
  343.1 3.4 copy.36
  349.5 3.4 copy.37
  366.7 3.2 gather_fusion
  369.9 3.2 fusion.54
  373.2 3.4 copy.36
  379.6 3.4 copy.37
  396.7 3.2 gather_fusion
  400.0 3.2 fusion.54
  403.2 3.4 copy.36
  409.6 3.4 copy.37
  424.3 96.0 %all-gather.15.cloned.1.call-done = bf16[1536,3072]{0,1:T(8,128)(2,1)} async-done(((bf16[1536,192]{0,1:T(8,128)(2,1)}), bf16[1536,3072]{0,1:T(8,128)(2,1)}) %all-gather.15.cloned.1.call-update) | async-done | bytes 9437200 | tf_op jit(solution)/shard_map/all_gather | solution.py:124
  520.4 6.9 %convolution_convert_fusion = bf16[1536,192]{0,1:T(8,128)(2,1)} fusion(bf16[1536,3072]{0,1:T(8,128)(2,1)} %all-gather.15.cloned.1.call-done, bf16[3072,192]{1,0:T(8,128)(2,1)} %all-gather.17.cloned.1.call-done), kind=kOutput, calls=%fused_computation.49 | convolution fusion | flops 1812234240 | bytes 11206656 | tf_op jit(solution)/shard_map/dot_general | solution.py:125
  (161 shorter events, 63.7 us)
Async XLA Ops:
  6.5 70.9 %all-gather.9.cloned.1.call-start = ((), (), s32[]{:S(2)}) async-start(), calls=%async_computation.1 | async-start | bytes 1671168 | tf_op jit(solution)/shard_map/all_gather | solution.py:83
  7.3 170.9 %all-gather.7.cloned.1.call-start = ((), (), s32[]{:S(2)}) async-start(), calls=%async_computation | async-start | bytes 10027008 | tf_op jit(solution)/shard_map/all_gather | solution.py:57
  8.0 234.7 %all-gather.11.cloned.1.call-start = ((), (), s32[]{:S(2)}) async-start(), calls=%async_computation.2 | async-start | bytes 1671168 | tf_op jit(solution)/shard_map/all_gather | solution.py:84
  8.7 307.2 %all-gather.13.cloned.1.call-start = ((), (), s32[]{:S(2)}) async-start(), calls=%async_computation.3 | async-start | bytes 1671168 | tf_op jit(solution)/shard_map/all_gather | solution.py:82
  9.3 415.0 %all-gather.17.cloned.1.call-start = ((), (), s32[]{:S(2)}) async-start(), calls=%async_computation.5 | async-start | bytes 1671168 | tf_op jit(solution)/shard_map/all_gather | solution.py:85
  9.9 510.5 %all-gather.15.cloned.1.call-start = ((), (), s32[]{:S(2)}) async-start(), calls=%async_computation.4 | async-start | bytes 10027008 | tf_op jit(solution)/shard_map/all_gather | solution.py:124
  250.1 73.1 %copy-start.1 = (bf16[1,1536,384]{1,2,0:T(8,128)(2,1)}, bf16[1,1536,384]{1,2,0:T(8,128)(2,1)S(1)}, u32[]{:S(2)}) copy-start(bf16[1,1536,384]{1,2,0:T(8,128)(2,1)S(1)} %maximum_bitcast_fusion) | copy-start | bytes 3538948
  250.1 75.3 %collective-permute-start.1 = (bf16[1,1536,384]{1,2,0:T(8,128)(2,1)S(1)}, bf16[1,1536,384]{1,2,0:T(8,128)(2,1)}, u32[]{:S(2)}, u32[]{:S(2)}) collective-permute-start(bf16[1,1536,384]{1,2,0:T(8,128)(2,1)S(1)} %maximum_bitcast_fusion), channel_id=1, source_target_pairs={{16,0},{32,16},{48,32},{64,48},{80,64},{96,80},{112,96},{128,112},... | collective-permute-start | bytes 3538952 | tf_op jit(solution)/shard_map/ppermute | solution.py:26
  251.4 74.0 %collective-permute-start = (bf16[1,1536,384]{1,2,0:T(8,128)(2,1)S(1)}, bf16[1,1536,384]{1,2,0:T(8,128)(2,1)}, u32[]{:S(2)}, u32[]{:S(2)}) collective-permute-start(bf16[1,1536,384]{1,2,0:T(8,128)(2,1)S(1)} %maximum_bitcast_fusion), channel_id=1, source_target_pairs={{0,16},{16,32},{32,48},{48,64},{64,80},{80,96},{96,112},{112,128},... | collective-permute-start | bytes 3538952 | tf_op jit(solution)/shard_map/ppermute | solution.py:23
  331.5 3.1 copy-start.4
  355.8 2.1 copy-start.2
  357.9 1.9 copy-start
  357.9 1.9 copy-start.3
  361.5 3.1 copy-start.4
  385.9 2.0 copy-start.2
  387.9 1.9 copy-start
  387.9 1.9 copy-start.3
  389.9 1.7 copy-start.5
  391.6 3.1 copy-start.4
  415.9 2.0 copy-start.2
  418.0 1.9 copy-start
  418.0 1.9 copy-start.3
  419.9 1.7 copy-start.5
  419.9 1.7 copy-start.7
  (6 other events, 9.3 us)
Sparse Core Ops, SparseCore 0:
  9.4 67.9 all-gather.8
  80.4 97.6 all-gather.6
  180.2 62.3 all-gather.10
  244.6 71.3 all-gather.12
  317.9 67.7 all-gather.16
  424.4 95.9 all-gather.14
where the time goes:
time: 535 us; the launch traced here: 534 us
  waiting for transfers between devices  380 us (71%)
  local copies, waits for them, and re-layouts  78.2 us (15%)
  matrix products  37 us (7%)
  other arithmetic  16.3 us (3%)
  between operations  13.6 us (3%)
  starting transfers between devices  6.49 us (1%)
    all_gather x1, waiting for transfers between devices, block_tokens(): return lax.all_gather(tokens, 'head', axis=0, tiled=True)  101 us
    all_gather x1, waiting for transfers between devices, on_device(): all_heads = lax.all_gather(outputs, 'head', axis=1, tiled=True)  96 us
    all_gather x1, waiting for transfers between devices, on_device(): lax.all_gather(w_key, 'context', axis=0, tiled=True)  63.8 us
    all_gather x1, waiting for transfers between devices, on_device(): lax.all_gather(w_query, 'context', axis=0, tiled=True)  59.5 us
    all_gather x1, waiting for transfers between devices, on_device(): lax.all_gather(w_value, 'context', axis=0, tiled=True)  56.7 us
    while x48, local copies, waits for them, and re-layouts  20.5 us
    dot_general x2, matrix products, normed(): raw = jnp.dot(rows_x, weight, preferred_element_type=jnp.float32)  14.6 us
  transfers between devices with their start and end apart: 8, of which 5 were waited for; matrix products, arithmetic and copies ran while one was open for 23% of the time, Pallas kernels for 0%

commit v1 on v0

v1 whole, which is shorter than its diff:
```python
import functools

import jax
import jax.numpy as jnp
from jax import lax
from jax.experimental import pallas as pl
from jax.experimental.pallas import tpu as pltpu
from jax.sharding import PartitionSpec as P

HEAD_DIM = 64
FRAME_H = 30
FRAME_W = 45
TILES_W = 6
TILES = 24
SLOTS = 1536
KT = 8
SIDE = 4
DEPTH = 16
D = 3072
MESH = pl.DeviceIdType.MESH
BF = jnp.bfloat16
F32 = jnp.float32


def place():
    g = lax.axis_index("guidance")
    z = lax.axis_index("context")
    h = lax.axis_index("head")
    return g, z, lax.div(h, SIDE), lax.rem(h, SIDE)


def at_xy(dx, dy):
    g, z, x, y = place()
    return (g, z, lax.rem(x + dx + SIDE, SIDE) * SIDE + lax.rem(y + dy + SIDE, SIDE))


def at_z(dz):
    g, z, x, y = place()
    return (g, lax.rem(z + dz + DEPTH, DEPTH), x * SIDE + y)


def sibling():
    g, z, x, y = place()
    return (1 - g, z, x * SIDE + y)


def send(src, dst, ssem, rsem, device):
    pltpu.make_async_remote_copy(
        src_ref=src, dst_ref=dst, send_sem=ssem, recv_sem=rsem, device_id=device, device_id_type=MESH
    ).start()


def wait_recv(dst, ssem, rsem):
    pltpu.make_async_remote_copy(
        src_ref=dst, dst_ref=dst, send_sem=ssem, recv_sem=rsem, device_id=sibling(), device_id_type=MESH
    ).wait_recv()


def wait_send(src, ssem, rsem):
    pltpu.make_async_remote_copy(
        src_ref=src, dst_ref=src, send_sem=ssem, recv_sem=rsem, device_id=sibling(), device_id_type=MESH
    ).wait_send()


def greet(partners):
    barrier = pltpu.get_barrier_semaphore()
    for partner in partners:
        pl.semaphore_signal(barrier, inc=1, device_id=partner, device_id_type=MESH)
    pl.semaphore_wait(barrier, len(partners))


def head_norm(raw, gain):
    lane_a = lax.broadcasted_iota(jnp.int32, (256, 256), 0) // HEAD_DIM
    lane_b = lax.broadcasted_iota(jnp.int32, (256, 256), 1) // HEAD_DIM
    pick = jnp.where(lane_a == lane_b, 1.0 / HEAD_DIM, 0.0).astype(BF)

    def mean(values):
        high = values.astype(BF)
        low = (values - high.astype(F32)).astype(BF)
        return jnp.dot(high, pick, preferred_element_type=F32) + jnp.dot(
            low, pick, preferred_element_type=F32
        )

    centred = raw - mean(raw)
    spread = mean(centred * centred)
    return centred * lax.rsqrt(spread + 1e-06) * gain


HALF = 48
COLS = D // 2


def project_kernel(
    tok_ref, wq_ref, wk_ref, wv_ref, wo_ref, qg_ref, kg_ref,
    q_ref, kv_ref, woq_ref,
    toks, wvk, tsend, trecv, zsend, zrecv, ssend, srecv, hsend, hrecv,
):
    g, z, x, y = place()
    greet([at_xy(1, 0), at_xy(-1, 0), at_xy(0, 1), at_xy(0, -1), at_z(1), at_z(-1), sibling()])
    sent = []

    def ship(src, dst, ssem, rsem, device):
        send(src, dst, ssem, rsem, device)
        sent.append((src, ssem, rsem))

    def axis_dev(p, second, step):
        along_x = (p == 0) != second
        return at_xy(step, 0) if along_x else at_xy(0, step)

    def cols(d):
        return pl.ds(d * COLS, COLS)

    def piece(p, ra, rb, d):
        return toks.at[p, ra, rb, :, cols(d)]

    def own(p, d):
        return tok_ref.at[pl.ds(p * HALF, HALF), cols(d)]

    def ship_first(p):
        for k, (d, step) in enumerate(((0, 1), (1, -1), (1, 1), (0, -1))):
            ra = 3 if step == 1 else 1
            ship(own(p, d), piece(p, ra, 0, d), tsend.at[p, 4, k], trecv.at[p, ra, 0, d], axis_dev(p, False, step))

    def ship_second(p, ra):
        for k, (d, step) in enumerate(((0, 1), (1, -1), (1, 1), (0, -1))):
            rb = 3 if step == 1 else 1
            src = own(p, d) if ra == 0 else piece(p, ra, 0, d)
            ship(src, piece(p, ra, rb, d), tsend.at[p, ra, k], trecv.at[p, ra, rb, d], axis_dev(p, True, step))

    def got(p, ra, rb, d):
        wait_recv(piece(p, ra, rb, d), tsend.at[p, 0, 0], trecv.at[p, ra, rb, d])

    def relay_first(p):
        got(p, 3, 0, 0)
        ship(piece(p, 3, 0, 0), piece(p, 2, 0, 0), tsend.at[p, 4, 4], trecv.at[p, 2, 0, 0], axis_dev(p, False, 1))
        got(p, 1, 0, 1)
        ship(piece(p, 1, 0, 1), piece(p, 2, 0, 1), tsend.at[p, 4, 5], trecv.at[p, 2, 0, 1], axis_dev(p, False, -1))

    def relay_second(p, ra):
        got(p, ra, 3, 0)
        ship(piece(p, ra, 3, 0), piece(p, ra, 2, 0), tsend.at[p, ra, 4], trecv.at[p, ra, 2, 0], axis_dev(p, True, 1))
        got(p, ra, 1, 1)
        ship(piece(p, ra, 1, 1), piece(p, ra, 2, 1), tsend.at[p, ra, 5], trecv.at[p, ra, 2, 1], axis_dev(p, True, -1))

    def rest_second(p, ra):
        got(p, ra, 3, 1)
        got(p, ra, 1, 0)
        got(p, ra, 2, 0)
        got(p, ra, 2, 1)

    def block(part, dz):
        ref = wvk if part == 0 else woq_ref
        return ref.at[lax.rem(z + dz + DEPTH, DEPTH), pl.ds(pl.multiple_of(g * 96, 96), 96), :]

    def other_block(part, dz):
        ref = wvk if part == 0 else woq_ref
        return ref.at[lax.rem(z + dz + DEPTH, DEPTH), pl.ds(pl.multiple_of((1 - g) * 96, 96), 96), :]

    def steps(part, way):
        return 8 if (part == 0) == (way == 0) else 7

    def ship_weights(part, way, s):
        dz = -s if way == 0 else s
        ship(block(part, dz), block(part, dz), zsend.at[part, way, s], zrecv.at[part, way, s], at_z(1 if way == 0 else -1))

    def weight_step(part, way, s):
        dz = -s if way == 0 else s
        if s > steps(part, way):
            return
        wait_recv(block(part, dz), zsend.at[part, way, 0], zrecv.at[part, way, s - 1])
        if s < steps(part, way):
            ship_weights(part, way, s)
        ship(block(part, dz), block(part, dz), ssend.at[part, way, s - 1], srecv.at[part, way, s - 1], sibling())

    def weight_round(s):
        for part in range(2):
            for way in range(2):
                weight_step(part, way, s)

    def weights_shared(part):
        for way in range(2):
            for s in range(1, steps(part, way) + 1):
                dz = -s if way == 0 else s
                wait_recv(other_block(part, dz), ssend.at[part, way, 0], srecv.at[part, way, s - 1])

    wvk[z] = jnp.concatenate([wv_ref[...], wk_ref[...]], axis=1)
    woq_ref[z] = jnp.concatenate([wo_ref[...], wq_ref[...]], axis=1)
    for part in range(2):
        for way in range(2):
            ship_weights(part, way, 0)
        if part == 0:
            ship_first(0)
            ship_first(1)
    for p in range(2):
        toks[p, 0, 0] = tok_ref[pl.ds(p * HALF, HALF), :]

    lane = lax.broadcasted_iota(jnp.int32, (1, 256), 1)
    q_gain = jnp.concatenate([qg_ref[...]] * 4, axis=1) * 0.125
    k_gain = jnp.concatenate([kg_ref[...]] * 4, axis=1)

    def rows_of(p, ra, rb):
        da, db = (x, y) if not isinstance(p, int) or p == 0 else (y, x)
        if not isinstance(p, int):
            a_x = jnp.where(p == 0, ra, rb)
            a_y = jnp.where(p == 0, rb, ra)
        else:
            a_x, a_y = (ra, rb) if p == 0 else (rb, ra)
        xs = lax.rem(x + a_x, SIDE)
        ys = lax.rem(y + a_y, SIDE)
        return pl.multiple_of(xs * 384 + ys * 96 + p * HALF, 16)

    def group(ra):
        def one(p, carry):
            rows = toks[p, ra].reshape(4 * HALF, D)
            raw_v = jnp.dot(rows, wvk[:, :, 0:128].reshape(D, 128), preferred_element_type=F32)
            raw_k = jnp.dot(rows, wvk[:, :, 128:384].reshape(D, 256), preferred_element_type=F32)
            raw_q = jnp.dot(rows, woq_ref[:, :, 128:384].reshape(D, 256), preferred_element_type=F32)
            key = jnp.where(lane >= HEAD_DIM, head_norm(raw_k, k_gain), raw_k)
            query = jnp.where(lane >= HEAD_DIM, head_norm(raw_q, q_gain), 0.0).astype(BF)
            keyval = jnp.concatenate([raw_v, key], axis=1).astype(BF)
            for rb in range(4):
                at = rows_of(p, ra, rb)
                q_ref[pl.ds(at, HALF), :] = query[rb * HALF : (rb + 1) * HALF]
                kv_ref[1, pl.ds(at, HALF), :] = keyval[rb * HALF : (rb + 1) * HALF]
            return carry

        lax.fori_loop(0, 2, one, 0)
        for p in range(2):
            for rb in range(4):
                here = pl.ds(rows_of(p, ra, rb), HALF)
                for way in range(2):
                    ship(
                        kv_ref.at[1, here, :], kv_ref.at[2 * way, here, :],
                        hsend.at[p, ra, rb, way], hrecv.at[p, ra, rb, way], at_z(1 - 2 * way),
                    )

    weight_round(1)
    for p in range(2):
        relay_first(p)
    for p in range(2):
        ship_second(p, 0)
    weight_round(2)
    weight_round(3)
    for p in range(2):
        got(p, 3, 0, 1)
        got(p, 1, 0, 0)
        ship_second(p, 3)
    weight_round(4)
    for p in range(2):
        relay_second(p, 0)
    weight_round(5)
    for p in range(2):
        ship_second(p, 1)
    weight_round(6)
    for p in range(2):
        got(p, 2, 0, 0)
        got(p, 2, 0, 1)
    for p in range(2):
        relay_second(p, 3)
    weight_round(7)
    for p in range(2):
        ship_second(p, 2)
    weight_round(8)
    for p in range(2):
        rest_second(p, 0)
    weights_shared(0)
    weights_shared(1)
    group(0)
    for p in range(2):
        relay_second(p, 1)
        rest_second(p, 3)
    group(3)
    for p in range(2):
        relay_second(p, 2)
        rest_second(p, 1)
    group(1)
    for p in range(2):
        rest_second(p, 2)
    group(2)
    for src, ssem, rsem in sent:
        wait_send(src, ssem, rsem)
    for ra in range(4):
        for p in range(2):
            for rb in range(4):
                here = pl.ds(rows_of(p, ra, rb), HALF)
                for way in range(2):
                    wait_recv(kv_ref.at[2 * way, here, :], hsend.at[0, 0, 0, 0], hrecv.at[p, ra, rb, way])


def project(tokens, w_query, w_key, w_value, w_out, q_gain, k_gain):
    vmem = pl.BlockSpec(memory_space=pltpu.VMEM)
    sems = pltpu.SemaphoreType.DMA
    return pl.pallas_call(
        project_kernel,
        out_shape=(
            jax.ShapeDtypeStruct((SLOTS, 256), BF),
            jax.ShapeDtypeStruct((3, SLOTS, 384), BF),
            jax.ShapeDtypeStruct((DEPTH, 192, 384), BF),
        ),
        in_specs=[vmem] * 7,
        out_specs=(vmem,) * 3,
        scratch_shapes=[
            pltpu.VMEM((2, 4, 4, HALF, D), BF),
            pltpu.VMEM((DEPTH, 192, 384), BF),
            sems((2, 5, 6)), sems((2, 4, 4, 2)),
            sems((2, 2, 8)), sems((2, 2, 8)),
            sems((2, 2, 8)), sems((2, 2, 8)),
            sems((2, 4, 4, 2)), sems((2, 4, 4, 2)),
        ],
        compiler_params=pltpu.CompilerParams(
            collective_id=0, has_side_effects=True, vmem_limit_bytes=56 * 1024 * 1024
        ),
        name="project",
    )(tokens, w_query, w_key, w_value, w_out, q_gain[None, :], k_gain[None, :])


def attend_kernel(
    tiles_ref, count_ref, q_ref, kv_ref, woq_ref,
    out_ref,
    wos, att, gat, acc, outs, wsend, wrecv, vsend, vrecv, asend, arecv, ysend, yrecv, osend, orecv,
):
    g, z, x, y = place()
    greet([at_xy(1, 0), at_xy(-1, 0), at_xy(2, 0), at_xy(0, 1), at_xy(0, -1), sibling()])
    sent = []

    def ship(src, dst, ssem, rsem, device):
        send(src, dst, ssem, rsem, device)
        sent.append((src, ssem, rsem))

    def wout(ra, c, half):
        return wos.at[ra, pl.ds(c * 8, 8), pl.ds(pl.multiple_of(64 + half * 96, 32), 96), :]

    for c in range(2):
        for k, (step, ra) in enumerate(((1, 3), (-1, 1))):
            ship(
                woq_ref.at[pl.ds(c * 8, 8), pl.ds(pl.multiple_of(g * 96, 96), 96), pl.ds(0, 256)],
                wout(ra, c, g), wsend.at[ra, c], wrecv.at[ra, c], at_xy(step, 0),
            )

    def wout_got(ra, c):
        wait_recv(wout(ra, c, g), wsend.at[0, 0], wrecv.at[ra, c])
        if ra == 3 and c == 0:
            ship(wout(3, 0, g), wout(2, 0, g), wsend.at[2, 0], wrecv.at[2, 0], at_xy(1, 0))
        if ra == 1 and c == 1:
            ship(wout(1, 1, g), wout(2, 1, g), wsend.at[2, 1], wrecv.at[2, 1], at_xy(-1, 0))
        ship(wout(ra, c, g), wout(ra, c, g), vsend.at[ra, c], vrecv.at[ra, c], sibling())

    wos[:, :, 0:64, :] = jnp.zeros((4, DEPTH, 64, 256), BF)
    wos[0, :, 64:256, :] = woq_ref[:, :, 0:256]
    acc[...] = jnp.zeros_like(acc)

    lane = lax.broadcasted_iota(jnp.int32, (1, 256), 1)
    key_lane = lax.broadcasted_iota(jnp.int32, (1, KT * 64), 1)
    slot = lax.rem(key_lane, 64)
    rank = lax.div(key_lane, 64)
    low_row = lax.div(slot, 8) < FRAME_H - 24
    low_col = lax.rem(slot, 8) < FRAME_W - 40
    row_slot = lax.broadcasted_iota(jnp.int32, (64, 1), 0)

    def attend_tile(tile):
        queries = q_ref[pl.ds(pl.multiple_of(tile * 64, 64), 64), :]
        stacked = jnp.concatenate(
            [jnp.where(lax.div(lane, 64) == h + 1, queries, jnp.zeros_like(queries)) for h in range(3)], axis=0
        )
        count = count_ref[tile]
        near = []
        row_last = jnp.zeros_like(key_lane)
        col_last = jnp.zeros_like(key_lane)
        for j in range(KT):
            index = jnp.clip(tiles_ref[tile, j] - (z - 1) * TILES, 0, 3 * TILES - 1)
            near.append(kv_ref[index])
            within = lax.rem(index, TILES)
            here = rank == j
            row_last = jnp.where(here, (within >= 18).astype(jnp.int32), row_last)
            col_last = jnp.where(here, (lax.rem(within, TILES_W) == TILES_W - 1).astype(jnp.int32), col_last)
        near = jnp.concatenate(near, axis=0)
        keep = (rank < count) & ((row_last == 0) | low_row) & ((col_last == 0) | low_col)
        scores = lax.dot_general(
            stacked, near[:, 128:384], (((1,), (1,)), ((), ())), preferred_element_type=F32
        )
        scores = jnp.where(keep, scores, -1e30)
        top = jnp.max(scores, axis=-1, keepdims=True)
        weights = jnp.exp(scores - top).astype(BF)
        values = jnp.where(lane >= 192, jnp.ones((), BF), near[:, 0:256])
        mixed = jnp.dot(weights, values, preferred_element_type=F32)
        mixed = mixed / mixed[:, 192:193]
        result = jnp.where(
            lane < 64, mixed[0:64], jnp.where(lane < 128, mixed[64:128], mixed[128:192])
        )
        row, col = lax.div(tile, TILES_W), lax.rem(tile, TILES_W)
        alive = (row * 8 + lax.div(row_slot, 8) < FRAME_H) & (col * 8 + lax.rem(row_slot, 8) < FRAME_W)
        return jnp.where(alive, result, 0.0)

    def attend_row(k, row):
        def one(i, carry):
            left = attend_tile(row * TILES_W + i)
            right = pltpu.roll(attend_tile(row * TILES_W + 3 + i), 64, 1)
            middle = jnp.where(lane[:, 0:128] < 64, left[:, 128:256], right[:, 0:128])
            packed = jnp.concatenate([left[:, 0:128], middle, right[:, 128:256]], axis=1).astype(BF)
            att[k, pl.ds(pl.multiple_of(i * 64, 64), 64), :] = packed
            return carry

        lax.fori_loop(0, 3, one, 0)

    def piece(ra, rb, d):
        return gat.at[ra, rb, pl.ds(d * 96, 96), :]

    def ship_y(ra):
        for k, (d, step) in enumerate(((0, 1), (1, -1), (1, 1), (0, -1))):
            rb = 3 if step == 1 else 1
            src = att.at[0, pl.ds(d * 96, 96), :] if ra == 0 else piece(ra, 0, d)
            ship(src, piece(ra, rb, d), ysend.at[ra, k], yrecv.at[ra, rb, d], at_xy(0, step))

    def got_y(ra, rb, d):
        wait_recv(piece(ra, rb, d), ysend.at[0, 0], yrecv.at[ra, rb, d])

    def relay_y(ra):
        got_y(ra, 3, 0)
        ship(piece(ra, 3, 0), piece(ra, 2, 0), ysend.at[ra, 4], yrecv.at[ra, 2, 0], at_xy(0, 1))
        got_y(ra, 1, 1)
        ship(piece(ra, 1, 1), piece(ra, 2, 1), ysend.at[ra, 5], yrecv.at[ra, 2, 1], at_xy(0, -1))

    def rest_y(ra):
        got_y(ra, 3, 1)
        got_y(ra, 1, 0)
        got_y(ra, 2, 0)
        got_y(ra, 2, 1)

    def add_source(ra, rb, own=False):
        h = lax.rem(x + ra, SIDE) * SIDE + lax.rem(y + rb, SIDE)
        rows = att[0] if own else gat[ra, rb]
        for xi in range(4):
            acc[xi, 0:192, :] += jnp.dot(rows[:, 0:192], wos[xi, h, 64:256, :], preferred_element_type=F32)
            acc[xi, 192:384, :] += jnp.dot(rows[:, 128:384], wos[xi, h, :, :], preferred_element_type=F32)

    def ship_x(k):
        ship(att.at[k], gat.at[4 - k, 0], asend.at[k], arecv.at[4 - k], at_xy(k, 0))

    def got_x(ra):
        wait_recv(gat.at[ra, 0], asend.at[0], arecv.at[ra])

    attend_row(0, x)
    ship_y(0)
    attend_row(1, lax.rem(x + 1, SIDE))
    ship_x(1)
    wout_got(3, 0)
    wout_got(1, 1)
    attend_row(3, lax.rem(x + 3, SIDE))
    ship_x(3)
    wout_got(3, 1)
    wout_got(1, 0)
    relay_y(0)
    attend_row(2, lax.rem(x + 2, SIDE))
    ship_x(2)
    got_x(3)
    ship_y(3)
    got_x(1)
    ship_y(1)
    rest_y(0)
    relay_y(3)
    got_x(2)
    ship_y(2)
    wout_got(2, 0)
    wout_got(2, 1)
    for ra in range(1, 4):
        for c in range(2):
            wait_recv(wout(ra, c, 1 - g), vsend.at[0, 0], vrecv.at[ra, c])
    add_source(0, 0, True)
    relay_y(1)

    def add_row(ra, first):
        def one(rb, carry):
            add_source(ra, rb)
            return carry

        lax.fori_loop(first, 4, one, 0)

    add_row(0, 1)
    rest_y(3)
    relay_y(2)
    add_row(3, 0)
    rest_y(1)
    add_row(1, 0)
    rest_y(2)
    add_row(2, 0)
    for xi in (2, 1, 3, 0):
        if xi == 0:
            outs[0] = acc[0].astype(BF)
        else:
            att_out = acc[xi].astype(BF)
            outs[4 + xi] = att_out
            ship(outs.at[4 + xi], outs.at[4 - xi], osend.at[xi], orecv.at[4 - xi], at_xy(xi, 0))
    for ra in (0, 3, 1, 2):
        if ra:
            wait_recv(outs.at[ra], osend.at[0], orecv.at[ra])
        at = pl.multiple_of(lax.rem(x + ra, SIDE) * 384, 384)
        out_ref[pl.ds(at, 384), :] = outs[ra][:, 0:192]
    for src, ssem, rsem in sent:
        wait_send(src, ssem, rsem)


def attend_and_project(key_tiles, key_count, query, keyval, woq):
    vmem = pl.BlockSpec(memory_space=pltpu.VMEM)
    smem = pl.BlockSpec(memory_space=pltpu.SMEM)
    sems = pltpu.SemaphoreType.DMA
    return pl.pallas_call(
        attend_kernel,
        out_shape=jax.ShapeDtypeStruct((SLOTS, 192), BF),
        in_specs=[smem, smem, vmem, vmem, vmem],
        out_specs=vmem,
        scratch_shapes=[
            pltpu.VMEM((4, DEPTH, 256, 256), BF),
            pltpu.VMEM((4, 192, 384), BF),
            pltpu.VMEM((4, 4, 192, 384), BF),
            pltpu.VMEM((4, 384, 256), F32),
            pltpu.VMEM((8, 384, 256), BF),
            sems((4, 2)), sems((4, 2)),
            sems((4, 2)), sems((4, 2)),
            sems((4,)), sems((4,)),
            sems((4, 6)), sems((4, 4, 2)),
            sems((4,)), sems((4,)),
        ],
        compiler_params=pltpu.CompilerParams(
            collective_id=1, has_side_effects=True, vmem_limit_bytes=56 * 1024 * 1024
        ),
        name="attend",
    )(key_tiles, key_count, query, keyval, woq)


def on_device(tokens, w_query, w_key, w_value, w_out, q_gain, k_gain, key_tiles, key_count):
    query, keyval, woq = project(tokens, w_query, w_key, w_value, w_out, q_gain, k_gain)
    return attend_and_project(key_tiles, key_count, query, keyval.reshape(3 * TILES, 64, 384), woq)


def solution(mesh):
    in_specs = (
        P(("guidance", "context", "head"), None),
        P("context", "head"),
        P("context", "head"),
        P("context", "head"),
        P("context", "head"),
        P(),
        P(),
        P("context", None),
        P("context"),
    )
    out_specs = P(("guidance", "context"), "head")
    return jax.shard_map(
        on_device, mesh=mesh, in_specs=in_specs, out_specs=out_specs, check_vma=False
    )
```

time: 535 us -> 152 us (0.28)
  waiting for transfers between devices: 380 us -> 0 us
  Pallas kernels: 0 us -> 149 us
  local copies, waits for them, and re-layouts: 78.2 us -> 3.56 us
  matrix products: 37 us -> 0 us
  other arithmetic: 16.3 us -> 0 us
  between operations: 13.6 us -> 0.02 us
  starting transfers between devices: 6.49 us -> 0 us
    all_gather x6 -> x0, waiting for transfers between devices: 377 us -> none  [the longest x1 101 us: block_tokens(): return lax.all_gather(tokens, 'head', axis=0, tiled=True)]
    pallas_call x0 -> x2, Pallas kernels: none -> 149 us  [the longest x1 83.8 us: project(): pl.pallas_call(project_kernel, out_shape=(jax.ShapeDtypeStruct((SLOTS, 25...]
    dot_general x10 -> x0, matrix products: 37 us -> none  [the longest x2 14.6 us: normed(): raw = jnp.dot(rows_x, weight, preferred_element_type=jnp.float32)]
    reshape x8 -> x0, local copies, waits for them, and re-layouts: 22.1 us -> none  [the longest x3 8.93 us: attend_block(): gathered[..., width:].reshape(block, KT * area, heads_here, HEAD_DIM)]
    while x48 -> x0, local copies, waits for them, and re-layouts: 20.5 us -> none
    slice x3 -> x0, local copies, waits for them, and re-layouts: 9.72 us -> none  [attend_block(): keys = gathered[..., :width].reshape(block, KT * area, heads_here, HEAD_DIM)]
    gather x3 -> x0, local copies, waits for them, and re-layouts: 9.68 us -> none  [attend_block(): gathered = window_tiles[lists]]
    ppermute x2 -> x0, starting transfers between devices: 6.3 us -> none  [the longest x1 5.01 us: padded(): lax.ppermute(lax.slice_in_dim(block, block.shape[dim] - width, None, axis...]
  transfers between devices with their start and end apart: 8 -> 0, of which waited for: 5 -> 0; matrix products, arithmetic and copies ran while one was open for 23% -> 0% of each run, Pallas kernels for 0% -> 0%
where the time goes in v1:
time: 152 us
  Pallas kernels  149 us (98%)
  local copies, waits for them, and re-layouts  3.56 us (2%)
    pallas_call x1, Pallas kernels, project(): pl.pallas_call(project_kernel, out_shape=(jax.ShapeDtypeStruct((SLOTS, 25...  83.8 us
    pallas_call x1, Pallas kernels, attend_and_project(): pl.pallas_call(attend_kernel, out_shape=jax.ShapeDtypeStruct((SLOTS, 192)...  64.7 us

profile of v1, /device:TPU:1, one launch (start us, length us, event | category | flops | bytes accessed | tf_op | source)
XLA Modules:
  0.0 152.2 jit_solution(1683351450393584740)
XLA Ops:
  0.0 1.4 copy.10.tiles_ref
  1.4 83.8 %project.1 = (bf16[1536,256]{1,0:T(8,128)(2,1)}, bf16[3,1536,384]{2,1,0:T(8,128)(2,1)}, bf16[16,192,384]{2,1,0:T(8,128)(2,1)}) custom-call(bf16[96,3072]{1,0:T(8,128)(2,1)} %tok_ref.1, bf16[192,192]{1,0:T(8,128)(2,1)} %wq_ref.1, bf16[192,192]{1,0:T(8,128)(2,1)} %wk_ref.1, bf16[192,192]{1,0:T(8,128)(2,1)} %wv_ref.1, bf16[192,192]{1,0:T(8,128)(2,1)} %wo_ref.1, ...), custom_call_target="tpu_custom_call" | custom-call | tf_op jit(solution)/shard_map/project/pallas_call | solution.py:293
  85.2 64.7 %attend.1 = bf16[1536,192]{1,0:T(8,128)(2,1)} custom-call(s32[24,8]{1,0:T(8,128)} %copy.10.tiles_ref, s32[24]{0:T(128)} %count_ref.1, bf16[1536,256]{1,0:T(8,128)(2,1)} %get-tuple-element.8.q_ref, bf16[72,64,384]{2,1,0:T(8,128)(2,1)} %bitcast.3, bf16[16,192,384]{2,1,0:T(8,128)(2,1)} %get-tuple-element.10.woq_ref), custom_call_target="tpu_custom_call" | custom-call | tf_op jit(solution)/shard_map/attend/pallas_call | solution.py:506
  150.0 2.2 %copy.11 = bf16[1536,192]{0,1:T(8,128)(2,1)} copy(bf16[1536,192]{1,0:T(8,128)(2,1)} %attend.1) | data formatting | bytes 1179648 | tf_op jit(solution)/shard_map/attend/pallas_call | solution.py:506

commit v2 on v1

v2 whole, which is shorter than its diff:
```python
import jax
import jax.numpy as jnp
from jax import lax
from jax.experimental import pallas as pl
from jax.experimental.pallas import tpu as pltpu
from jax.sharding import PartitionSpec as P

HEAD_DIM = 64
FRAME_H = 30
FRAME_W = 45
TILES_W = 6
TILES = 24
SLOTS = 1536
KT = 8
SIDE = 4
DEPTH = 16
D = 3072
MESH = pl.DeviceIdType.MESH
BF = jnp.bfloat16
F32 = jnp.float32


def place():
    g = lax.axis_index("guidance")
    z = lax.axis_index("context")
    h = lax.axis_index("head")
    return g, z, lax.div(h, SIDE), lax.rem(h, SIDE)


def at_xy(dx, dy):
    g, z, x, y = place()
    return (g, z, lax.rem(x + dx + SIDE, SIDE) * SIDE + lax.rem(y + dy + SIDE, SIDE))


def at_z(dz):
    g, z, x, y = place()
    return (g, lax.rem(z + dz + DEPTH, DEPTH), x * SIDE + y)


def sibling():
    g, z, x, y = place()
    return (1 - g, z, x * SIDE + y)


def send(src, dst, ssem, rsem, device):
    pltpu.make_async_remote_copy(
        src_ref=src, dst_ref=dst, send_sem=ssem, recv_sem=rsem, device_id=device, device_id_type=MESH
    ).start()


def wait_recv(dst, ssem, rsem):
    pltpu.make_async_remote_copy(
        src_ref=dst, dst_ref=dst, send_sem=ssem, recv_sem=rsem, device_id=sibling(), device_id_type=MESH
    ).wait_recv()


def wait_send(src, ssem, rsem):
    pltpu.make_async_remote_copy(
        src_ref=src, dst_ref=src, send_sem=ssem, recv_sem=rsem, device_id=sibling(), device_id_type=MESH
    ).wait_send()


def greet(partners):
    barrier = pltpu.get_barrier_semaphore()
    for partner in partners:
        pl.semaphore_signal(barrier, inc=1, device_id=partner, device_id_type=MESH)
    pl.semaphore_wait(barrier, len(partners))


def head_norm(raw, gain):
    lane_a = lax.broadcasted_iota(jnp.int32, (256, 256), 0) // HEAD_DIM
    lane_b = lax.broadcasted_iota(jnp.int32, (256, 256), 1) // HEAD_DIM
    pick = jnp.where(lane_a == lane_b, 1.0 / HEAD_DIM, 0.0).astype(BF)

    def mean(values):
        high = values.astype(BF)
        low = (values - high.astype(F32)).astype(BF)
        return jnp.dot(high, pick, preferred_element_type=F32) + jnp.dot(
            low, pick, preferred_element_type=F32
        )

    centred = raw - mean(raw)
    spread = mean(centred * centred)
    return centred * lax.rsqrt(spread + 1e-06) * gain


HALF = 48
COLS = D // 2
WAYS = ((0, 1), (1, -1))
PARTS = ((0, 0, 48, 8), (0, 48, 48, 8), (1, 0, 96, 7), (2, 0, 96, 8))


def block_kernel(
    tiles_hbm, count_hbm, tok_ref, wq_ref, wk_ref, wv_ref, wo_ref, qg_ref, kg_ref,
    out_ref,
    tiles_ref, count_ref, toks, wvk, woq, query_ref, kv, wos, att, gat, acc, outs,
    csem, tsend, trecv, zsend, zrecv, ssend, srecv, hsend, hrecv,
    wsend, wrecv, vsend, vrecv, asend, arecv, ysend, yrecv, osend, orecv,
):
    g, z, x, y = place()
    lists = pltpu.make_async_copy(tiles_hbm, tiles_ref, csem.at[0])
    counts = pltpu.make_async_copy(count_hbm, count_ref, csem.at[1])
    lists.start()
    counts.start()
    greet([
        at_xy(1, 0), at_xy(-1, 0), at_xy(2, 0), at_xy(0, 1), at_xy(0, -1), at_z(1), at_z(-1), sibling()
    ])
    sent = []

    def ship(src, dst, ssem, rsem, device):
        send(src, dst, ssem, rsem, device)
        sent.append((src, ssem, rsem))

    def drain():
        for src, ssem, rsem in sent:
            wait_send(src, ssem, rsem)
        sent.clear()

    def axis_dev(p, second, step):
        along_x = (p == 0) != second
        return at_xy(step, 0) if along_x else at_xy(0, step)

    def piece(p, ra, rb, d):
        return toks.at[ra, p, rb, :, pl.ds(d * COLS, COLS)]

    def landing(p, rnd, rel, d):
        return piece(p, rel, 0, d) if rnd == 4 else piece(p, rnd, rel, d)

    def own(p, d):
        return tok_ref.at[pl.ds(p * HALF, HALF), pl.ds(d * COLS, COLS)]

    def arrival(p, rnd, rel, d):
        return trecv.at[p, rel, 0, d] if rnd == 4 else trecv.at[p, rnd, rel, d]

    def start(rnd, k):
        for p in range(2):
            for i, (d, step) in enumerate(WAYS):
                d = d ^ k
                src = own(p, d) if rnd in (0, 4) else piece(p, rnd, 0, d)
                rel = 3 if step == 1 else 1
                ship(src, landing(p, rnd, rel, d), tsend.at[p, rnd, 2 * k + i], arrival(p, rnd, rel, d),
                     axis_dev(p, rnd != 4, step))

    def got(p, rnd, rel, d):
        wait_recv(landing(p, rnd, rel, d), tsend.at[p, 0, 0], arrival(p, rnd, rel, d))

    def relay(rnd):
        for p in range(2):
            for i, (d, step) in enumerate(WAYS):
                rel = 3 if step == 1 else 1
                got(p, rnd, rel, d)
                ship(landing(p, rnd, rel, d), landing(p, rnd, 2, d), tsend.at[p, rnd, 4 + i],
                     arrival(p, rnd, 2, d), axis_dev(p, rnd != 4, step))

    def near_rest(rnd):
        for p in range(2):
            got(p, rnd, 3, 1)
            got(p, rnd, 1, 0)

    def far(rnd):
        for p in range(2):
            got(p, rnd, 2, 0)
            got(p, rnd, 2, 1)

    def block(part, dz, half):
        which, first, height, _ = PARTS[part]
        at = lax.rem(z + dz + DEPTH, DEPTH)
        rows = pl.ds(pl.multiple_of(half * 96 + first, 16), height)
        if which == 0:
            return wvk.at[at, rows, :]
        if which == 1:
            return woq.at[at, rows, :]
        return wos.at[0, at, pl.ds(pl.multiple_of(64 + half * 96, 32), height), pl.ds(0, 128)]

    def steps(part, way):
        count = PARTS[part][3]
        return count if way == 0 else 15 - count

    def ship_weights(part, way, s):
        dz = -s if way == 0 else s
        ship(block(part, dz, g), block(part, dz, g), zsend.at[part, way, s], zrecv.at[part, way, s],
             at_z(1 if way == 0 else -1))

    def weight_round(s, parts):
        for part in parts:
            for way in range(2):
                if s > steps(part, way):
                    continue
                dz = -s if way == 0 else s
                here = block(part, dz, g)
                wait_recv(here, zsend.at[part, way, 0], zrecv.at[part, way, s - 1])
                if s < steps(part, way):
                    ship_weights(part, way, s)
                ship(here, here, ssend.at[part, way, s - 1], srecv.at[part, way, s - 1], sibling())

    def weights_shared(parts):
        for part in parts:
            for way in range(2):
                for s in range(1, steps(part, way) + 1):
                    dz = -s if way == 0 else s
                    wait_recv(block(part, dz, 1 - g), ssend.at[part, way, 0], srecv.at[part, way, s - 1])

    start(4, 0)
    wvk[z] = jnp.concatenate([wv_ref[...], wk_ref[...]], axis=1)
    for part in (0, 1):
        for way in range(2):
            ship_weights(part, way, 0)
    start(4, 1)
    both = jnp.concatenate([wo_ref[...], wq_ref[...]], axis=1)
    woq[z] = both[:, 128:384]
    wos[0, z, 64:256, 0:128] = both[:, 0:128]
    for part in (2, 3):
        for way in range(2):
            ship_weights(part, way, 0)
    start(0, 0)
    for p in range(2):
        toks[0, p, 0] = tok_ref[pl.ds(p * HALF, HALF), :]
    wos[:, :, 0:64, :] = jnp.zeros((4, DEPTH, 64, 256), BF)
    acc[...] = jnp.zeros_like(acc)

    lane = lax.broadcasted_iota(jnp.int32, (1, 256), 1)
    q_gain = jnp.concatenate([qg_ref[...]] * 4, axis=1) * 0.125
    k_gain = jnp.concatenate([kg_ref[...]] * 4, axis=1)

    def unit(p, ra, rb):
        a_x, a_y = (ra, rb) if p == 0 else (rb, ra)
        return lax.rem(x + a_x, SIDE) * 24 + lax.rem(y + a_y, SIDE) * 6 + p * 3

    def group(ra):
        rows = toks[ra].reshape(8 * HALF, D)
        raw = jnp.dot(rows, wvk[...].reshape(D, 384), preferred_element_type=F32)
        raw_q = jnp.dot(rows, woq[...].reshape(D, 256), preferred_element_type=F32)
        raw_k = raw[:, 128:384]
        key = jnp.where(lane >= HEAD_DIM, head_norm(raw_k, k_gain), raw_k)
        query = jnp.where(lane >= HEAD_DIM, head_norm(raw_q, q_gain), 0.0).astype(BF)
        keyval = jnp.concatenate([raw[:, 0:128], key], axis=1).astype(BF)
        for p in range(2):
            for rb in range(4):
                at = unit(p, ra, rb)
                part = (p * 4 + rb) * HALF
                query_ref[pl.ds(pl.multiple_of(at * 16, 16), HALF), :] = query[part : part + HALF]
                kv[pl.ds(96 + at, 3)] = keyval[part : part + HALF].reshape(3, 16, 384)
                for way in range(2):
                    ship(kv.at[pl.ds(96 + at, 3)], kv.at[pl.ds(192 * way + at, 3)],
                         hsend.at[p, ra, rb, way], hrecv.at[p, ra, rb, way], at_z(1 - 2 * way))

    def halo(ra):
        for p in range(2):
            for rb in range(4):
                at = unit(p, ra, rb)
                for way in range(2):
                    wait_recv(kv.at[pl.ds(192 * way + at, 3)], hsend.at[0, 0, 0, 0], hrecv.at[p, ra, rb, way])

    def wout(ra, c, half):
        return wos.at[ra, pl.ds(c * 8, 8), pl.ds(pl.multiple_of(64 + half * 96, 32), 96), :]

    def wout_start():
        wos[0, :, 64:256, 128:256] = woq[:, :, 0:128]
        for c in range(2):
            for step, ra in ((1, 3), (-1, 1)):
                ship(wout(0, c, g), wout(ra, c, g), wsend.at[ra, c], wrecv.at[ra, c], at_xy(step, 0))

    def wout_got(ra, c):
        wait_recv(wout(ra, c, g), wsend.at[0, 0], wrecv.at[ra, c])
        if ra == 3 and c == 0:
            ship(wout(3, 0, g), wout(2, 0, g), wsend.at[2, 0], wrecv.at[2, 0], at_xy(1, 0))
        if ra == 1 and c == 1:
            ship(wout(1, 1, g), wout(2, 1, g), wsend.at[2, 1], wrecv.at[2, 1], at_xy(-1, 0))
        ship(wout(ra, c, g), wout(ra, c, g), vsend.at[ra, c], vrecv.at[ra, c], sibling())

    early, late = (0, 1, 2), (3,)
    weight_round(1, early)
    relay(4)
    start(0, 1)
    weight_round(2, early)
    near_rest(4)
    start(3, 0)
    weight_round(3, early)
    weight_round(4, early)
    relay(0)
    start(3, 1)
    weight_round(5, early)
    start(1, 0)
    weight_round(6, early)
    near_rest(0)
    relay(3)
    start(1, 1)
    weight_round(7, early)
    weight_round(8, early)
    far(4)
    far(0)
    weights_shared(early)
    group(0)
    start(2, 0)
    weight_round(1, late)
    weight_round(2, late)
    relay(1)
    start(2, 1)
    weight_round(3, late)
    weight_round(4, late)
    near_rest(3)
    far(3)
    group(3)
    weight_round(5, late)
    weight_round(6, late)
    relay(2)
    weight_round(7, late)
    near_rest(1)
    far(1)
    group(1)
    weight_round(8, late)
    weights_shared(late)
    near_rest(2)
    wout_start()
    far(2)
    group(2)
    halo(0)
    halo(3)
    lists.wait()
    counts.wait()

    key_lane = lax.broadcasted_iota(jnp.int32, (1, KT * 64), 1)
    slot = lax.rem(key_lane, 64)
    rank = lax.div(key_lane, 64)
    low_row = lax.div(slot, 8) < FRAME_H - 24
    low_col = lax.rem(slot, 8) < FRAME_W - 40
    row_slot = lax.broadcasted_iota(jnp.int32, (64, 1), 0)

    def attend_tile(tile):
        queries = query_ref[pl.ds(pl.multiple_of(tile * 64, 64), 64), :]
        stacked = jnp.concatenate(
            [jnp.where(lax.div(lane, 64) == h + 1, queries, jnp.zeros_like(queries)) for h in range(3)], axis=0
        )
        count = count_ref[tile]
        near = []
        row_last = jnp.zeros_like(key_lane)
        col_last = jnp.zeros_like(key_lane)
        for j in range(KT):
            index = jnp.clip(tiles_ref[tile, j] - (z - 1) * TILES, 0, 3 * TILES - 1)
            near += [kv[4 * index + i] for i in range(4)]
            within = lax.rem(index, TILES)
            here = rank == j
            row_last = jnp.where(here, (within >= 18).astype(jnp.int32), row_last)
            col_last = jnp.where(here, (lax.rem(within, TILES_W) == TILES_W - 1).astype(jnp.int32), col_last)
        near = jnp.concatenate(near, axis=0)
        keep = (rank < count) & ((row_last == 0) | low_row) & ((col_last == 0) | low_col)
        scores = lax.dot_general(
            stacked, near[:, 128:384], (((1,), (1,)), ((), ())), preferred_element_type=F32
        )
        scores = jnp.where(keep, scores, -1e30)
        top = jnp.max(scores, axis=-1, keepdims=True)
        weights = jnp.exp(scores - top).astype(BF)
        values = jnp.where(lane >= 192, jnp.ones((), BF), near[:, 0:256])
        mixed = jnp.dot(weights, values, preferred_element_type=F32)
        mixed = mixed / mixed[:, 192:193]
        result = jnp.where(
            lane < 64, mixed[0:64], jnp.where(lane < 128, mixed[64:128], mixed[128:192])
        )
        row, col = lax.div(tile, TILES_W), lax.rem(tile, TILES_W)
        alive = (row * 8 + lax.div(row_slot, 8) < FRAME_H) & (col * 8 + lax.rem(row_slot, 8) < FRAME_W)
        return jnp.where(alive, result, 0.0)

    def pack(left, right):
        right = pltpu.roll(right, 64, 1)
        middle = jnp.where(lane[:, 0:128] < 64, left[:, 128:256], right[:, 0:128])
        return jnp.concatenate([left[:, 0:128], middle, right[:, 128:256]], axis=1).astype(BF)

    def attend_row(k):
        row = lax.rem(x + k, SIDE)

        def one(i, carry):
            at = row * TILES_W + i
            att[k, pl.ds(pl.multiple_of(i * 64, 64), 64), :] = pack(attend_tile(at), attend_tile(at + 3))
            return carry

        lax.fori_loop(0, 3, one, 0)

    def mixed_piece(ra, rb, d):
        return gat.at[ra, rb, pl.ds(d * 96, 96), :]

    def start_y(ra):
        for k in range(2):
            for i, (d, step) in enumerate(WAYS):
                d = d ^ k
                src = att.at[0, pl.ds(d * 96, 96), :] if ra == 0 else mixed_piece(ra, 0, d)
                rb = 3 if step == 1 else 1
                ship(src, mixed_piece(ra, rb, d), ysend.at[ra, 2 * k + i], yrecv.at[ra, rb, d], at_xy(0, step))

    def got_y(ra, rb, d):
        wait_recv(mixed_piece(ra, rb, d), ysend.at[0, 0], yrecv.at[ra, rb, d])

    def relay_y(ra):
        for i, (d, step) in enumerate(WAYS):
            rb = 3 if step == 1 else 1
            got_y(ra, rb, d)
            ship(mixed_piece(ra, rb, d), mixed_piece(ra, 2, d), ysend.at[ra, 4 + i], yrecv.at[ra, 2, d],
                 at_xy(0, step))

    def rest_y(ra):
        got_y(ra, 3, 1)
        got_y(ra, 1, 0)
        got_y(ra, 2, 0)
        got_y(ra, 2, 1)

    def add_source(ra, rb, rows):
        h = lax.rem(x + ra, SIDE) * SIDE + lax.rem(y + rb, SIDE)
        for xi in range(4):
            acc[xi, 0:192, :] += jnp.dot(rows[:, 0:192], wos[xi, h, 64:256, :], preferred_element_type=F32)
            acc[xi, 192:384, :] += jnp.dot(rows[:, 128:384], wos[xi, h, :, :], preferred_element_type=F32)

    def add_row(ra, first):
        def one(rb, carry):
            add_source(ra, rb, gat[ra, rb])
            return carry

        lax.fori_loop(first, 4, one, 0)

    def start_x(k):
        ship(att.at[k], gat.at[4 - k, 0], asend.at[k], arecv.at[4 - k], at_xy(k, 0))

    def got_x(ra):
        wait_recv(gat.at[ra, 0], asend.at[0], arecv.at[ra])

    halo(1)
    halo(2)
    attend_row(0)
    start_y(0)
    attend_row(1)
    start_x(1)
    wout_got(3, 0)
    wout_got(1, 1)
    attend_row(3)
    start_x(3)
    wout_got(3, 1)
    wout_got(1, 0)
    relay_y(0)
    attend_row(2)
    start_x(2)
    drain()
    got_x(3)
    start_y(3)
    got_x(1)
    start_y(1)
    rest_y(0)
    relay_y(3)
    got_x(2)
    start_y(2)
    wout_got(2, 0)
    wout_got(2, 1)
    relay_y(1)
    for ra in range(1, 4):
        for c in range(2):
            wait_recv(wout(ra, c, 1 - g), vsend.at[0, 0], vrecv.at[ra, c])
    add_source(0, 0, att[0])
    add_row(0, 1)
    rest_y(3)
    relay_y(2)
    add_row(3, 0)
    rest_y(1)
    add_row(1, 0)
    drain()
    rest_y(2)
    add_row(2, 0)
    for xi in (2, 1, 3):
        outs[xi] = pack(acc[xi, 0:192, :], acc[xi, 192:384, :])
        ship(outs.at[xi], outs.at[8 - xi], osend.at[xi], orecv.at[4 - xi], at_xy(xi, 0))
    here = pl.multiple_of(x * 384, 384)
    out_ref[pl.ds(here, 384), :] = acc[0, :, 0:192].astype(BF)
    for ra in (3, 1, 2):
        wait_recv(outs.at[4 + ra], osend.at[0], orecv.at[ra])
        at = pl.multiple_of(lax.rem(x + ra, SIDE) * 384, 384)
        packed = outs[4 + ra]
        out_ref[pl.ds(at, 192), :] = packed[:, 0:192]
        right = pltpu.roll(packed[:, 128:384].astype(F32), 192, 1)
        out_ref[pl.ds(at + 192, 192), :] = right[:, 0:192].astype(BF)
    drain()


def on_device(tokens, w_query, w_key, w_value, w_out, q_gain, k_gain, key_tiles, key_count):
    vmem = pl.BlockSpec(memory_space=pltpu.VMEM)
    anywhere = pl.BlockSpec(memory_space=pl.ANY)
    sems = pltpu.SemaphoreType.DMA
    return pl.pallas_call(
        block_kernel,
        out_shape=jax.ShapeDtypeStruct((SLOTS, 192), BF),
        in_specs=[anywhere] * 2 + [vmem] * 7,
        out_specs=vmem,
        scratch_shapes=[
            pltpu.SMEM((TILES, KT), jnp.int32),
            pltpu.SMEM((TILES,), jnp.int32),
            pltpu.VMEM((4, 2, 4, HALF, D), BF),
            pltpu.VMEM((DEPTH, 192, 384), BF),
            pltpu.VMEM((DEPTH, 192, 256), BF),
            pltpu.VMEM((SLOTS, 256), BF),
            pltpu.VMEM((288, 16, 384), BF),
            pltpu.VMEM((4, DEPTH, 256, 256), BF),
            pltpu.VMEM((4, 192, 384), BF),
            pltpu.VMEM((4, 4, 192, 384), BF),
            pltpu.VMEM((4, 384, 256), F32),
            pltpu.VMEM((8, 192, 384), BF),
            sems((2,)),
            sems((2, 5, 6)), sems((2, 4, 4, 2)),
            sems((4, 2, 8)), sems((4, 2, 8)),
            sems((4, 2, 8)), sems((4, 2, 8)),
            sems((2, 4, 4, 2)), sems((2, 4, 4, 2)),
            sems((4, 2)), sems((4, 2)),
            sems((4, 2)), sems((4, 2)),
            sems((4,)), sems((4,)),
            sems((4, 6)), sems((4, 4, 2)),
            sems((4,)), sems((4,)),
        ],
        compiler_params=pltpu.CompilerParams(
            collective_id=0, has_side_effects=True, vmem_limit_bytes=56 * 1024 * 1024
        ),
        name="block_attention",
    )(key_tiles, key_count, tokens, w_query, w_key, w_value, w_out, q_gain[None, :], k_gain[None, :])


def solution(mesh):
    in_specs = (
        P(("guidance", "context", "head"), None),
        P("context", "head"),
        P("context", "head"),
        P("context", "head"),
        P("context", "head"),
        P(),
        P(),
        P("context", None),
        P("context"),
    )
    out_specs = P(("guidance", "context"), "head")
    return jax.shard_map(
        on_device, mesh=mesh, in_specs=in_specs, out_specs=out_specs, check_vma=False
    )
```

time: 152 us -> 152 us (level)
    pallas_call x2 -> x1, Pallas kernels: 149 us -> 148 us  [on_device(): pl.pallas_call(block_kernel, out_shape=jax.ShapeDtypeStruct((SLOTS, 192),...]
where the time goes in v2:
time: 152 us
  Pallas kernels  148 us (97%)
  local copies, waits for them, and re-layouts  3.56 us (2%)
    pallas_call x1, Pallas kernels, on_device(): pl.pallas_call(block_kernel, out_shape=jax.ShapeDtypeStruct((SLOTS, 192),...  148 us

profile of v2, /device:TPU:1, one launch (start us, length us, event | category | flops | bytes accessed | tf_op | source)
XLA Modules:
  0.0 151.9 jit_solution(10806872507604789255)
XLA Ops:
  0.0 1.4 copy.10.tiles_hbm
  1.4 148.4 %block_attention.1 = bf16[1536,192]{1,0:T(8,128)(2,1)} custom-call(s32[24,8]{1,0:T(8,128)} %copy.10.tiles_hbm, s32[24]{0:T(128)} %count_hbm.1, bf16[96,3072]{1,0:T(8,128)(2,1)} %tok_ref.1, bf16[192,192]{1,0:T(8,128)(2,1)} %wq_ref.1, bf16[192,192]{1,0:T(8,128)(2,1)} %wk_ref.1, bf16[192,192]{1,0:T(8,128)(2,1)} %wv_ref.1, bf16[192,192]{1,0:T(8,128)(2,1)} %wo_ref.1, ...), custom_call_target="tpu_custom_call" | custom-call | tf_op jit(solution)/shard_map/block_attention/pallas_call | solution.py:483
  149.7 2.2 %copy.11 = bf16[1536,192]{0,1:T(8,128)(2,1)} copy(bf16[1536,192]{1,0:T(8,128)(2,1)} %block_attention.1) | data formatting | bytes 1179648 | tf_op jit(solution)/shard_map/block_attention/pallas_call | solution.py:483

commit v3 on v2

--- a/solution.py
+++ b/solution.py
@@ -87,13 +87,15 @@
 HALF = 48
 COLS = D // 2
 WAYS = ((0, 1), (1, -1))
-PARTS = ((0, 0, 48, 8), (0, 48, 48, 8), (1, 0, 96, 7), (2, 0, 96, 8))
+STREAMS = 3
+ORDER = (0, 3, 1, 2)
+SLOT = {0: 0, 3: 1, 1: 2}
 
 
 def block_kernel(
     tiles_hbm, count_hbm, tok_ref, wq_ref, wk_ref, wv_ref, wo_ref, qg_ref, kg_ref,
     out_ref,
-    tiles_ref, count_ref, toks, wvk, woq, query_ref, kv, wos, att, gat, acc, outs,
+    tiles_ref, count_ref, close, distant, wall, query_ref, kv, wos, att, gat, acc, outs,
     csem, tsend, trecv, zsend, zrecv, ssend, srecv, hsend, hrecv,
     wsend, wrecv, vsend, vrecv, asend, arecv, ysend, yrecv, osend, orecv,
 ):
@@ -121,7 +123,9 @@
         return at_xy(step, 0) if along_x else at_xy(0, step)
 
     def piece(p, ra, rb, d):
-        return toks.at[ra, p, rb, :, pl.ds(d * COLS, COLS)]
+        at = ORDER.index(ra)
+        here = distant.at[at, p] if rb == 2 else close.at[at, p, SLOT[rb]]
+        return here.at[:, pl.ds(d * COLS, COLS)]
 
     def landing(p, rnd, rel, d):
         return piece(p, rel, 0, d) if rnd == 4 else piece(p, rnd, rel, d)
@@ -162,61 +166,52 @@
             got(p, rnd, 2, 0)
             got(p, rnd, 2, 1)
 
-    def block(part, dz, half):
-        which, first, height, _ = PARTS[part]
+    def block(stream, dz, half):
         at = lax.rem(z + dz + DEPTH, DEPTH)
-        rows = pl.ds(pl.multiple_of(half * 96 + first, 16), height)
-        if which == 0:
-            return wvk.at[at, rows, :]
-        if which == 1:
-            return woq.at[at, rows, :]
-        return wos.at[0, at, pl.ds(pl.multiple_of(64 + half * 96, 32), height), pl.ds(0, 128)]
-
-    def steps(part, way):
-        count = PARTS[part][3]
-        return count if way == 0 else 15 - count
-
-    def ship_weights(part, way, s):
+        return wall.at[at, pl.ds(pl.multiple_of(half * 96, 96), 96), pl.ds(stream * 256, 256)]
+
+    def steps(stream, way):
+        return 8 if (stream + way) % 2 == 0 else 7
+
+    def ship_weights(stream, way, s):
         dz = -s if way == 0 else s
-        ship(block(part, dz, g), block(part, dz, g), zsend.at[part, way, s], zrecv.at[part, way, s],
+        ship(block(stream, dz, g), block(stream, dz, g), zsend.at[stream, way, s], zrecv.at[stream, way, s],
              at_z(1 if way == 0 else -1))
 
-    def weight_round(s, parts):
-        for part in parts:
+    def ship_stream(stream):
+        for way in range(2):
+            ship_weights(stream, way, 0)
+
+    def weight_round(s):
+        for stream in range(STREAMS):
             for way in range(2):
-                if s > steps(part, way):
+                if s > steps(stream, way):
                     continue
                 dz = -s if way == 0 else s
-                here = block(part, dz, g)
-                wait_recv(here, zsend.at[part, way, 0], zrecv.at[part, way, s - 1])
-                if s < steps(part, way):
-                    ship_weights(part, way, s)
-                ship(here, here, ssend.at[part, way, s - 1], srecv.at[part, way, s - 1], sibling())
-
-    def weights_shared(parts):
-        for part in parts:
+                here = block(stream, dz, g)
+                wait_recv(here, zsend.at[stream, way, 0], zrecv.at[stream, way, s - 1])
+                if s < steps(stream, way):
+                    ship_weights(stream, way, s)
+                ship(here, here, ssend.at[stream, way, s - 1], srecv.at[stream, way, s - 1], sibling())
+
+    def weights_shared():
+        for stream in range(STREAMS):
             for way in range(2):
-                for s in range(1, steps(part, way) + 1):
+                for s in range(1, steps(stream, way) + 1):
                     dz = -s if way == 0 else s
-                    wait_recv(block(part, dz, 1 - g), ssend.at[part, way, 0], srecv.at[part, way, s - 1])
+                    wait_recv(block(stream, dz, 1 - g), ssend.at[stream, way, 0], srecv.at[stream, way, s - 1])
 
     start(4, 0)
-    wvk[z] = jnp.concatenate([wv_ref[...], wk_ref[...]], axis=1)
-    for part in (0, 1):
-        for way in range(2):
-            ship_weights(part, way, 0)
+    wall[z, :, 0:384] = jnp.concatenate([wv_ref[...], wk_ref[...]], axis=1)
+    ship_stream(0)
     start(4, 1)
-    both = jnp.concatenate([wo_ref[...], wq_ref[...]], axis=1)
-    woq[z] = both[:, 128:384]
-    wos[0, z, 64:256, 0:128] = both[:, 0:128]
-    for part in (2, 3):
-        for way in range(2):
-            ship_weights(part, way, 0)
+    wall[z, :, 384:768] = jnp.concatenate([wo_ref[...], wq_ref[...]], axis=1)
+    ship_stream(1)
+    for p in range(2):
+        close[0, p, 0] = tok_ref[pl.ds(p * HALF, HALF), :]
+    wos[:, :, 0:64, :] = jnp.zeros((4, DEPTH, 64, 256), BF)
+    ship_stream(2)
     start(0, 0)
-    for p in range(2):
-        toks[0, p, 0] = tok_ref[pl.ds(p * HALF, HALF), :]
-    wos[:, :, 0:64, :] = jnp.zeros((4, DEPTH, 64, 256), BF)
-    acc[...] = jnp.zeros_like(acc)
 
     lane = lax.broadcasted_iota(jnp.int32, (1, 256), 1)
     q_gain = jnp.concatenate([qg_ref[...]] * 4, axis=1) * 0.125
@@ -226,23 +221,28 @@
         a_x, a_y = (ra, rb) if p == 0 else (rb, ra)
         return lax.rem(x + a_x, SIDE) * 24 + lax.rem(y + a_y, SIDE) * 6 + p * 3
 
-    def group(ra):
-        rows = toks[ra].reshape(8 * HALF, D)
-        raw = jnp.dot(rows, wvk[...].reshape(D, 384), preferred_element_type=F32)
-        raw_q = jnp.dot(rows, woq[...].reshape(D, 256), preferred_element_type=F32)
+    def group(rows, pieces):
+        raw = jnp.dot(rows, wall[:, :, 0:384].reshape(D, 384), preferred_element_type=F32)
+        raw_q = jnp.dot(rows, wall[:, :, 512:768].reshape(D, 256), preferred_element_type=F32)
         raw_k = raw[:, 128:384]
         key = jnp.where(lane >= HEAD_DIM, head_norm(raw_k, k_gain), raw_k)
         query = jnp.where(lane >= HEAD_DIM, head_norm(raw_q, q_gain), 0.0).astype(BF)
         keyval = jnp.concatenate([raw[:, 0:128], key], axis=1).astype(BF)
-        for p in range(2):
-            for rb in range(4):
-                at = unit(p, ra, rb)
-                part = (p * 4 + rb) * HALF
-                query_ref[pl.ds(pl.multiple_of(at * 16, 16), HALF), :] = query[part : part + HALF]
-                kv[pl.ds(96 + at, 3)] = keyval[part : part + HALF].reshape(3, 16, 384)
-                for way in range(2):
-                    ship(kv.at[pl.ds(96 + at, 3)], kv.at[pl.ds(192 * way + at, 3)],
-                         hsend.at[p, ra, rb, way], hrecv.at[p, ra, rb, way], at_z(1 - 2 * way))
+        for i, (p, ra, rb) in enumerate(pieces):
+            at = unit(p, ra, rb)
+            part = slice(i * HALF, (i + 1) * HALF)
+            query_ref[pl.ds(pl.multiple_of(at * 16, 16), HALF), :] = query[part]
+            kv[pl.ds(96 + at, 3)] = keyval[part].reshape(3, 16, 384)
+            for way in range(2):
+                ship(kv.at[pl.ds(96 + at, 3)], kv.at[pl.ds(192 * way + at, 3)],
+                     hsend.at[p, ra, rb, way], hrecv.at[p, ra, rb, way], at_z(1 - 2 * way))
+
+    def near_group(ra):
+        group(close[ORDER.index(ra)].reshape(6 * HALF, D), [(p, ra, rb) for p in range(2) for rb in SLOT])
+
+    def far_group(first, last):
+        group(distant[first:last].reshape((last - first) * 2 * HALF, D),
+              [(p, ORDER[at], 2) for at in range(first, last) for p in range(2)])
 
     def halo(ra):
         for p in range(2):
@@ -255,7 +255,7 @@
         return wos.at[ra, pl.ds(c * 8, 8), pl.ds(pl.multiple_of(64 + half * 96, 32), 96), :]
 
     def wout_start():
-        wos[0, :, 64:256, 128:256] = woq[:, :, 0:128]
+        wos[0, :, 64:256, :] = wall[:, :, 384:640]
         for c in range(2):
             for step, ra in ((1, 3), (-1, 1)):
                 ship(wout(0, c, g), wout(ra, c, g), wsend.at[ra, c], wrecv.at[ra, c], at_xy(step, 0))
@@ -268,54 +268,44 @@
             ship(wout(1, 1, g), wout(2, 1, g), wsend.at[2, 1], wrecv.at[2, 1], at_xy(-1, 0))
         ship(wout(ra, c, g), wout(ra, c, g), vsend.at[ra, c], vrecv.at[ra, c], sibling())
 
-    early, late = (0, 1, 2), (3,)
-    weight_round(1, early)
+    weight_round(1)
     relay(4)
     start(0, 1)
-    weight_round(2, early)
+    weight_round(2)
     near_rest(4)
     start(3, 0)
-    weight_round(3, early)
-    weight_round(4, early)
+    weight_round(3)
     relay(0)
     start(3, 1)
-    weight_round(5, early)
     start(1, 0)
-    weight_round(6, early)
-    near_rest(0)
+    weight_round(4)
+    weight_round(5)
+    weight_round(6)
     relay(3)
     start(1, 1)
-    weight_round(7, early)
-    weight_round(8, early)
     far(4)
-    far(0)
-    weights_shared(early)
-    group(0)
     start(2, 0)
-    weight_round(1, late)
-    weight_round(2, late)
+    weight_round(7)
+    weight_round(8)
+    weights_shared()
+    near_rest(0)
+    near_group(0)
     relay(1)
     start(2, 1)
-    weight_round(3, late)
-    weight_round(4, late)
     near_rest(3)
+    near_group(3)
+    near_rest(1)
+    near_group(1)
+    relay(2)
+    far(0)
     far(3)
-    group(3)
-    weight_round(5, late)
-    weight_round(6, late)
-    relay(2)
-    weight_round(7, late)
-    near_rest(1)
     far(1)
-    group(1)
-    weight_round(8, late)
-    weights_shared(late)
+    far_group(0, 3)
     near_rest(2)
     wout_start()
+    near_group(2)
     far(2)
-    group(2)
-    halo(0)
-    halo(3)
+    far_group(3, 4)
     lists.wait()
     counts.wait()
 
@@ -336,7 +326,7 @@
         row_last = jnp.zeros_like(key_lane)
         col_last = jnp.zeros_like(key_lane)
         for j in range(KT):
-            index = jnp.clip(tiles_ref[tile, j] - (z - 1) * TILES, 0, 3 * TILES - 1)
+            index = jnp.clip(tiles_ref[j, tile] - (z - 1) * TILES, 0, 3 * TILES - 1)
             near += [kv[4 * index + i] for i in range(4)]
             within = lax.rem(index, TILES)
             here = rank == j
@@ -402,11 +392,17 @@
         got_y(ra, 2, 0)
         got_y(ra, 2, 1)
 
-    def add_source(ra, rb, rows):
+    def add_source(ra, rb, rows, first=False):
         h = lax.rem(x + ra, SIDE) * SIDE + lax.rem(y + rb, SIDE)
         for xi in range(4):
-            acc[xi, 0:192, :] += jnp.dot(rows[:, 0:192], wos[xi, h, 64:256, :], preferred_element_type=F32)
-            acc[xi, 192:384, :] += jnp.dot(rows[:, 128:384], wos[xi, h, :, :], preferred_element_type=F32)
+            top = jnp.dot(rows[:, 0:192], wos[xi, h, 64:256, :], preferred_element_type=F32)
+            low = jnp.dot(rows[:, 128:384], wos[xi, h, :, :], preferred_element_type=F32)
+            if first:
+                acc[xi, 0:192, :] = top
+                acc[xi, 192:384, :] = low
+            else:
+                acc[xi, 0:192, :] += top
+                acc[xi, 192:384, :] += low
 
     def add_row(ra, first):
         def one(rb, carry):
@@ -421,37 +417,37 @@
     def got_x(ra):
         wait_recv(gat.at[ra, 0], asend.at[0], arecv.at[ra])
 
-    halo(1)
-    halo(2)
+    for ra in ORDER:
+        halo(ra)
     attend_row(0)
     start_y(0)
     attend_row(1)
     start_x(1)
-    wout_got(3, 0)
-    wout_got(1, 1)
     attend_row(3)
     start_x(3)
-    wout_got(3, 1)
-    wout_got(1, 0)
     relay_y(0)
     attend_row(2)
     start_x(2)
-    drain()
+    wout_got(3, 0)
+    wout_got(1, 1)
     got_x(3)
     start_y(3)
     got_x(1)
     start_y(1)
+    drain()
+    wout_got(3, 1)
+    wout_got(1, 0)
     rest_y(0)
     relay_y(3)
     got_x(2)
     start_y(2)
+    relay_y(1)
     wout_got(2, 0)
     wout_got(2, 1)
-    relay_y(1)
     for ra in range(1, 4):
         for c in range(2):
             wait_recv(wout(ra, c, 1 - g), vsend.at[0, 0], vrecv.at[ra, c])
-    add_source(0, 0, att[0])
+    add_source(0, 0, att[0], True)
     add_row(0, 1)
     rest_y(3)
     relay_y(2)
@@ -461,18 +457,15 @@
     drain()
     rest_y(2)
     add_row(2, 0)
+    def result(xs):
+        return out_ref.at[:, pl.ds(pl.multiple_of(xs * 384, 128), 384)]
+
     for xi in (2, 1, 3):
-        outs[xi] = pack(acc[xi, 0:192, :], acc[xi, 192:384, :])
-        ship(outs.at[xi], outs.at[8 - xi], osend.at[xi], orecv.at[4 - xi], at_xy(xi, 0))
-    here = pl.multiple_of(x * 384, 384)
-    out_ref[pl.ds(here, 384), :] = acc[0, :, 0:192].astype(BF)
+        outs[xi] = acc[xi].T[0:192].astype(BF)
+        ship(outs.at[xi], result(x), osend.at[xi], orecv.at[4 - xi], at_xy(xi, 0))
+    out_ref[:, pl.ds(pl.multiple_of(x * 384, 128), 384)] = acc[0].T[0:192].astype(BF)
     for ra in (3, 1, 2):
-        wait_recv(outs.at[4 + ra], osend.at[0], orecv.at[ra])
-        at = pl.multiple_of(lax.rem(x + ra, SIDE) * 384, 384)
-        packed = outs[4 + ra]
-        out_ref[pl.ds(at, 192), :] = packed[:, 0:192]
-        right = pltpu.roll(packed[:, 128:384].astype(F32), 192, 1)
-        out_ref[pl.ds(at + 192, 192), :] = right[:, 0:192].astype(BF)
+        wait_recv(result(lax.rem(x + ra, SIDE)), osend.at[0], orecv.at[ra])
     drain()
 
 
@@ -482,26 +475,26 @@
     sems = pltpu.SemaphoreType.DMA
     return pl.pallas_call(
         block_kernel,
-        out_shape=jax.ShapeDtypeStruct((SLOTS, 192), BF),
+        out_shape=jax.ShapeDtypeStruct((192, SLOTS), BF),
         in_specs=[anywhere] * 2 + [vmem] * 7,
         out_specs=vmem,
         scratch_shapes=[
-            pltpu.SMEM((TILES, KT), jnp.int32),
+            pltpu.SMEM((KT, TILES), jnp.int32),
             pltpu.SMEM((TILES,), jnp.int32),
-            pltpu.VMEM((4, 2, 4, HALF, D), BF),
-            pltpu.VMEM((DEPTH, 192, 384), BF),
-            pltpu.VMEM((DEPTH, 192, 256), BF),
+            pltpu.VMEM((4, 2, 3, HALF, D), BF),
+            pltpu.VMEM((4, 2, HALF, D), BF),
+            pltpu.VMEM((DEPTH, 192, 768), BF),
             pltpu.VMEM((SLOTS, 256), BF),
             pltpu.VMEM((288, 16, 384), BF),
             pltpu.VMEM((4, DEPTH, 256, 256), BF),
             pltpu.VMEM((4, 192, 384), BF),
             pltpu.VMEM((4, 4, 192, 384), BF),
             pltpu.VMEM((4, 384, 256), F32),
-            pltpu.VMEM((8, 192, 384), BF),
+            pltpu.VMEM((4, 192, 384), BF),
             sems((2,)),
             sems((2, 5, 6)), sems((2, 4, 4, 2)),
-            sems((4, 2, 8)), sems((4, 2, 8)),
-            sems((4, 2, 8)), sems((4, 2, 8)),
+            sems((STREAMS, 2, 8)), sems((STREAMS, 2, 8)),
+            sems((STREAMS, 2, 8)), sems((STREAMS, 2, 8)),
             sems((2, 4, 4, 2)), sems((2, 4, 4, 2)),
             sems((4, 2)), sems((4, 2)),
             sems((4, 2)), sems((4, 2)),
@@ -513,7 +506,7 @@
             collective_id=0, has_side_effects=True, vmem_limit_bytes=56 * 1024 * 1024
         ),
         name="block_attention",
-    )(key_tiles, key_count, tokens, w_query, w_key, w_value, w_out, q_gain[None, :], k_gain[None, :])
+    )(key_tiles.T, key_count, tokens, w_query, w_key, w_value, w_out, q_gain[None, :], k_gain[None, :]).T
 
 
 def solution(mesh):

time: 152 us -> 126 us (0.83)
  Pallas kernels: 148 us -> 124 us
  local copies, waits for them, and re-layouts: 3.56 us -> 1.92 us
    pallas_call x1, Pallas kernels: 148 us -> 124 us  [on_device(): pl.pallas_call(block_kernel, out_shape=jax.ShapeDtypeStruct((192, SLOTS),...]
    pallas_call x1 -> x0, local copies, waits for them, and re-layouts: 2.21 us -> none  [on_device(): pl.pallas_call(block_kernel, out_shape=jax.ShapeDtypeStruct((SLOTS, 192),...]
where the time goes in v3:
time: 126 us
  Pallas kernels  124 us (98%)
  local copies, waits for them, and re-layouts  1.92 us (2%)
    pallas_call x1, Pallas kernels, on_device(): pl.pallas_call(block_kernel, out_shape=jax.ShapeDtypeStruct((192, SLOTS),...  124 us

profile of v3, /device:TPU:1, one launch (start us, length us, event | category | flops | bytes accessed | tf_op | source)
XLA Modules:
  0.0 126.2 jit_solution(12255876175329417988)
XLA Ops:
  0.0 124.3 %block_attention.1 = bf16[192,1536]{1,0:T(8,128)(2,1)} custom-call(s32[8,24]{1,0:T(8,128)} %bitcast.5, s32[24]{0:T(128)} %count_hbm.1, bf16[96,3072]{1,0:T(8,128)(2,1)} %tok_ref.1, bf16[192,192]{1,0:T(8,128)(2,1)} %wq_ref.1, bf16[192,192]{1,0:T(8,128)(2,1)} %wk_ref.1, bf16[192,192]{1,0:T(8,128)(2,1)} %wv_ref.1, bf16[192,192]{1,0:T(8,128)(2,1)} %wo_ref.1, ...), custom_call_target="tpu_custom_call" | custom-call | tf_op jit(solution)/shard_map/block_attention/pallas_call | solution.py:476
  124.3 1.9 %copy.11 = bf16[1536,192]{0,1:T(8,128)(2,1)} copy(bf16[1536,192]{0,1:T(8,128)(2,1)} %bitcast.4) | data formatting | bytes 1179648

commit v4 on v3

--- a/solution.py
+++ b/solution.py
@@ -87,7 +87,7 @@
 HALF = 48
 COLS = D // 2
 WAYS = ((0, 1), (1, -1))
-STREAMS = 3
+STREAMS = 6
 ORDER = (0, 3, 1, 2)
 SLOT = {0: 0, 3: 1, 1: 2}
 
@@ -95,7 +95,7 @@
 def block_kernel(
     tiles_hbm, count_hbm, tok_ref, wq_ref, wk_ref, wv_ref, wo_ref, qg_ref, kg_ref,
     out_ref,
-    tiles_ref, count_ref, close, distant, wall, query_ref, kv, wos, att, gat, acc, outs,
+    tiles_ref, count_ref, close, distant, wall, query_ref, kv, wos, pairs, att, gat, acc, outs,
     csem, tsend, trecv, zsend, zrecv, ssend, srecv, hsend, hrecv,
     wsend, wrecv, vsend, vrecv, asend, arecv, ysend, yrecv, osend, orecv,
 ):
@@ -168,7 +168,8 @@
 
     def block(stream, dz, half):
         at = lax.rem(z + dz + DEPTH, DEPTH)
-        return wall.at[at, pl.ds(pl.multiple_of(half * 96, 96), 96), pl.ds(stream * 256, 256)]
+        rows = pl.ds(pl.multiple_of(half * 96 + stream % 2 * 48, 16), 48)
+        return wall.at[at, rows, pl.ds(stream // 2 * 256, 256)]
 
     def steps(stream, way):
         return 8 if (stream + way) % 2 == 0 else 7
@@ -204,14 +205,16 @@
     start(4, 0)
     wall[z, :, 0:384] = jnp.concatenate([wv_ref[...], wk_ref[...]], axis=1)
     ship_stream(0)
+    ship_stream(1)
     start(4, 1)
     wall[z, :, 384:768] = jnp.concatenate([wo_ref[...], wq_ref[...]], axis=1)
-    ship_stream(1)
+    ship_stream(2)
+    ship_stream(3)
     for p in range(2):
         close[0, p, 0] = tok_ref[pl.ds(p * HALF, HALF), :]
     wos[:, :, 0:64, :] = jnp.zeros((4, DEPTH, 64, 256), BF)
-    ship_stream(2)
-    start(0, 0)
+    ship_stream(4)
+    ship_stream(5)
 
     lane = lax.broadcasted_iota(jnp.int32, (1, 256), 1)
     q_gain = jnp.concatenate([qg_ref[...]] * 4, axis=1) * 0.125
@@ -252,28 +255,54 @@
                     wait_recv(kv.at[pl.ds(192 * way + at, 3)], hsend.at[0, 0, 0, 0], hrecv.at[p, ra, rb, way])
 
     def wout(ra, c, half):
-        return wos.at[ra, pl.ds(c * 8, 8), pl.ds(pl.multiple_of(64 + half * 96, 32), 96), :]
-
-    def wout_start():
+        if c < 4:
+            rows = pl.ds(pl.multiple_of(64 + half * 96, 32), 96)
+            return wos.at[ra, pl.ds(c * 4, 4), rows, pl.ds(0, 128)]
+        return pairs.at[ra, pl.ds((c - 4) * 4, 4), pl.ds(pl.multiple_of(half * 96, 32), 96), :]
+
+    def swap(block):
+        return pltpu.roll(block.astype(F32).reshape(8 * 192, 128), 64, 1).reshape(8, 192, 128).astype(BF)
+
+    def wout_own():
         wos[0, :, 64:256, :] = wall[:, :, 384:640]
-        for c in range(2):
-            for step, ra in ((1, 3), (-1, 1)):
-                ship(wout(0, c, g), wout(ra, c, g), wsend.at[ra, c], wrecv.at[ra, c], at_xy(step, 0))
-
-    def wout_got(ra, c):
+        lower = lane[:, 0:128].reshape(1, 1, 128) < 64
+        pairs[0] = jnp.where(lower, wall[0:8, :, 512:640], swap(wall[8:16, :, 512:640]))
+
+    def wout_start(k):
+        for c in range(6):
+            step, ra = ((1, 3), (-1, 1))[(c in (2, 3, 5)) ^ k]
+            ship(wout(0, c, g), wout(ra, c, g), wsend.at[ra, c], wrecv.at[ra, c], at_xy(step, 0))
+
+    def wout_pass(ra, c):
         wait_recv(wout(ra, c, g), wsend.at[0, 0], wrecv.at[ra, c])
-        if ra == 3 and c == 0:
-            ship(wout(3, 0, g), wout(2, 0, g), wsend.at[2, 0], wrecv.at[2, 0], at_xy(1, 0))
-        if ra == 1 and c == 1:
-            ship(wout(1, 1, g), wout(2, 1, g), wsend.at[2, 1], wrecv.at[2, 1], at_xy(-1, 0))
         ship(wout(ra, c, g), wout(ra, c, g), vsend.at[ra, c], vrecv.at[ra, c], sibling())
 
+    def wout_relay():
+        for c in range(6):
+            step, ra = ((1, 3), (-1, 1))[c in (2, 3, 5)]
+            wout_pass(ra, c)
+            ship(wout(ra, c, g), wout(2, c, g), wsend.at[2, c], wrecv.at[2, c], at_xy(step, 0))
+
+    def wout_rest():
+        for c in range(6):
+            wout_pass(1 if c in (0, 1, 4) else 3, c)
+        for c in range(6):
+            wout_pass(2, c)
+
+    def wout_finish():
+        for ra in range(1, 4):
+            for c in range(6):
+                wait_recv(wout(ra, c, 1 - g), vsend.at[0, 0], vrecv.at[ra, c])
+            wos[ra, 0:8, 64:256, 128:256] = pairs[ra]
+            wos[ra, 8:16, 64:256, 128:256] = swap(pairs[ra])
+
     weight_round(1)
+    start(0, 0)
     relay(4)
+    near_rest(4)
     start(0, 1)
+    start(3, 0)
     weight_round(2)
-    near_rest(4)
-    start(3, 0)
     weight_round(3)
     relay(0)
     start(3, 1)
@@ -281,9 +310,9 @@
     weight_round(4)
     weight_round(5)
     weight_round(6)
+    far(4)
     relay(3)
     start(1, 1)
-    far(4)
     start(2, 0)
     weight_round(7)
     weight_round(8)
@@ -297,15 +326,20 @@
     near_rest(1)
     near_group(1)
     relay(2)
+    wout_own()
+    wout_start(0)
     far(0)
     far(3)
     far(1)
     far_group(0, 3)
     near_rest(2)
-    wout_start()
     near_group(2)
     far(2)
+    wout_relay()
+    wout_start(1)
     far_group(3, 4)
+    for ra in ORDER:
+        halo(ra)
     lists.wait()
     counts.wait()
 
@@ -417,8 +451,6 @@
     def got_x(ra):
         wait_recv(gat.at[ra, 0], asend.at[0], arecv.at[ra])
 
-    for ra in ORDER:
-        halo(ra)
     attend_row(0)
     start_y(0)
     attend_row(1)
@@ -428,29 +460,22 @@
     relay_y(0)
     attend_row(2)
     start_x(2)
-    wout_got(3, 0)
-    wout_got(1, 1)
+    wout_rest()
+    drain()
     got_x(3)
     start_y(3)
     got_x(1)
     start_y(1)
-    drain()
-    wout_got(3, 1)
-    wout_got(1, 0)
-    rest_y(0)
-    relay_y(3)
     got_x(2)
     start_y(2)
+    relay_y(3)
     relay_y(1)
-    wout_got(2, 0)
-    wout_got(2, 1)
-    for ra in range(1, 4):
-        for c in range(2):
-            wait_recv(wout(ra, c, 1 - g), vsend.at[0, 0], vrecv.at[ra, c])
+    wout_finish()
     add_source(0, 0, att[0], True)
+    rest_y(0)
     add_row(0, 1)
+    relay_y(2)
     rest_y(3)
-    relay_y(2)
     add_row(3, 0)
     rest_y(1)
     add_row(1, 0)
@@ -487,6 +512,7 @@
             pltpu.VMEM((SLOTS, 256), BF),
             pltpu.VMEM((288, 16, 384), BF),
             pltpu.VMEM((4, DEPTH, 256, 256), BF),
+            pltpu.VMEM((4, 8, 192, 128), BF),
             pltpu.VMEM((4, 192, 384), BF),
             pltpu.VMEM((4, 4, 192, 384), BF),
             pltpu.VMEM((4, 384, 256), F32),
@@ -496,8 +522,8 @@
             sems((STREAMS, 2, 8)), sems((STREAMS, 2, 8)),
             sems((STREAMS, 2, 8)), sems((STREAMS, 2, 8)),
             sems((2, 4, 4, 2)), sems((2, 4, 4, 2)),
-            sems((4, 2)), sems((4, 2)),
-            sems((4, 2)), sems((4, 2)),
+            sems((4, 6)), sems((4, 6)),
+            sems((4, 6)), sems((4, 6)),
             sems((4,)), sems((4,)),
             sems((4, 6)), sems((4, 4, 2)),
             sems((4,)), sems((4,)),

time: 126 us -> 127 us (level); the launches traced: 126 us -> 125 us
  no operation moved by 1% of the time
where the time goes in v4:
time: 127 us; the launch traced here: 125 us
  Pallas kernels  123 us (97%)
  local copies, waits for them, and re-layouts  1.92 us (2%)
    pallas_call x1, Pallas kernels, on_device(): pl.pallas_call(block_kernel, out_shape=jax.ShapeDtypeStruct((192, SLOTS),...  123 us

profile of v4, /device:TPU:1, one launch (start us, length us, event | category | flops | bytes accessed | tf_op | source)
XLA Modules:
  0.0 125.2 jit_solution(16983146867241234193)
XLA Ops:
  0.0 123.3 %block_attention.1 = bf16[192,1536]{1,0:T(8,128)(2,1)} custom-call(s32[8,24]{1,0:T(8,128)} %bitcast.5, s32[24]{0:T(128)} %count_hbm.1, bf16[96,3072]{1,0:T(8,128)(2,1)} %tok_ref.1, bf16[192,192]{1,0:T(8,128)(2,1)} %wq_ref.1, bf16[192,192]{1,0:T(8,128)(2,1)} %wk_ref.1, bf16[192,192]{1,0:T(8,128)(2,1)} %wv_ref.1, bf16[192,192]{1,0:T(8,128)(2,1)} %wo_ref.1, ...), custom_call_target="tpu_custom_call" | custom-call | tf_op jit(solution)/shard_map/block_attention/pallas_call | solution.py:501
  123.3 1.9 %copy.11 = bf16[1536,192]{0,1:T(8,128)(2,1)} copy(bf16[1536,192]{0,1:T(8,128)(2,1)} %bitcast.4) | data formatting | bytes 1179648

commit v5 on v4

--- a/solution.py
+++ b/solution.py
@@ -299,20 +299,20 @@
     weight_round(1)
     start(0, 0)
     relay(4)
+    start(0, 1)
+    weight_round(2)
     near_rest(4)
-    start(0, 1)
     start(3, 0)
-    weight_round(2)
     weight_round(3)
+    weight_round(4)
     relay(0)
     start(3, 1)
     start(1, 0)
-    weight_round(4)
     weight_round(5)
     weight_round(6)
-    far(4)
     relay(3)
     start(1, 1)
+    far(4)
     start(2, 0)
     weight_round(7)
     weight_round(8)
@@ -426,9 +426,9 @@
         got_y(ra, 2, 0)
         got_y(ra, 2, 1)
 
-    def add_source(ra, rb, rows, first=False):
+    def add_source(ra, rb, rows, first=False, targets=range(4)):
         h = lax.rem(x + ra, SIDE) * SIDE + lax.rem(y + rb, SIDE)
-        for xi in range(4):
+        for xi in targets:
             top = jnp.dot(rows[:, 0:192], wos[xi, h, 64:256, :], preferred_element_type=F32)
             low = jnp.dot(rows[:, 128:384], wos[xi, h, :, :], preferred_element_type=F32)
             if first:
@@ -481,14 +481,21 @@
     add_row(1, 0)
     drain()
     rest_y(2)
-    add_row(2, 0)
     def result(xs):
         return out_ref.at[:, pl.ds(pl.multiple_of(xs * 384, 128), 384)]
 
+    def finish(xi):
+        def one(rb, carry):
+            add_source(2, rb, gat[2, rb], targets=(xi,))
+            return carry
+
+        lax.fori_loop(0, 4, one, 0)
+        return acc[xi].T[0:192].astype(BF)
+
     for xi in (2, 1, 3):
-        outs[xi] = acc[xi].T[0:192].astype(BF)
+        outs[xi] = finish(xi)
         ship(outs.at[xi], result(x), osend.at[xi], orecv.at[4 - xi], at_xy(xi, 0))
-    out_ref[:, pl.ds(pl.multiple_of(x * 384, 128), 384)] = acc[0].T[0:192].astype(BF)
+    out_ref[:, pl.ds(pl.multiple_of(x * 384, 128), 384)] = finish(0)
     for ra in (3, 1, 2):
         wait_recv(result(lax.rem(x + ra, SIDE)), osend.at[0], orecv.at[ra])
     drain()

time: 127 us -> 122 us (0.961)
  the two profiles are of different devices: /device:TPU:1 before, /device:TPU:2 now
where the time goes in v5:
time: 122 us
  Pallas kernels  120 us (98%)
  local copies, waits for them, and re-layouts  1.92 us (2%)
    pallas_call x1, Pallas kernels, on_device(): pl.pallas_call(block_kernel, out_shape=jax.ShapeDtypeStruct((192, SLOTS),...  120 us

profile of v5, /device:TPU:2, one launch (start us, length us, event | category | flops | bytes accessed | tf_op | source)
XLA Modules:
  0.0 122.0 jit_solution(14217119705275482154)
XLA Ops:
  0.0 120.1 %block_attention.1 = bf16[192,1536]{1,0:T(8,128)(2,1)} custom-call(s32[8,24]{1,0:T(8,128)} %bitcast.5, s32[24]{0:T(128)} %count_hbm.1, bf16[96,3072]{1,0:T(8,128)(2,1)} %tok_ref.1, bf16[192,192]{1,0:T(8,128)(2,1)} %wq_ref.1, bf16[192,192]{1,0:T(8,128)(2,1)} %wk_ref.1, bf16[192,192]{1,0:T(8,128)(2,1)} %wv_ref.1, bf16[192,192]{1,0:T(8,128)(2,1)} %wo_ref.1, ...), custom_call_target="tpu_custom_call" | custom-call | tf_op jit(solution)/shard_map/block_attention/pallas_call | solution.py:508
  120.1 1.9 %copy.11 = bf16[1536,192]{0,1:T(8,128)(2,1)} copy(bf16[1536,192]{0,1:T(8,128)(2,1)} %bitcast.4) | data formatting | bytes 1179648

commit v6 on v5

--- a/solution.py
+++ b/solution.py
@@ -113,10 +113,10 @@
         send(src, dst, ssem, rsem, device)
         sent.append((src, ssem, rsem))
 
-    def drain():
-        for src, ssem, rsem in sent:
+    def drain(count):
+        for src, ssem, rsem in sent[:count]:
             wait_send(src, ssem, rsem)
-        sent.clear()
+        del sent[:count]
 
     def axis_dev(p, second, step):
         along_x = (p == 0) != second
@@ -326,6 +326,7 @@
     near_rest(1)
     near_group(1)
     relay(2)
+    projected = len(sent)
     wout_own()
     wout_start(0)
     far(0)
@@ -338,8 +339,10 @@
     wout_relay()
     wout_start(1)
     far_group(3, 4)
+    drain(projected)
     for ra in ORDER:
         halo(ra)
+    shared = len(sent)
     lists.wait()
     counts.wait()
 
@@ -376,7 +379,7 @@
         weights = jnp.exp(scores - top).astype(BF)
         values = jnp.where(lane >= 192, jnp.ones((), BF), near[:, 0:256])
         mixed = jnp.dot(weights, values, preferred_element_type=F32)
-        mixed = mixed / mixed[:, 192:193]
+        mixed = mixed * (1.0 / mixed[:, 192:193])
         result = jnp.where(
             lane < 64, mixed[0:64], jnp.where(lane < 128, mixed[64:128], mixed[128:192])
         )
@@ -461,13 +464,13 @@
     attend_row(2)
     start_x(2)
     wout_rest()
-    drain()
     got_x(3)
     start_y(3)
     got_x(1)
     start_y(1)
     got_x(2)
     start_y(2)
+    drain(shared)
     relay_y(3)
     relay_y(1)
     wout_finish()
@@ -479,7 +482,7 @@
     add_row(3, 0)
     rest_y(1)
     add_row(1, 0)
-    drain()
+    drain(len(sent))
     rest_y(2)
     def result(xs):
         return out_ref.at[:, pl.ds(pl.multiple_of(xs * 384, 128), 384)]
@@ -498,7 +501,7 @@
     out_ref[:, pl.ds(pl.multiple_of(x * 384, 128), 384)] = finish(0)
     for ra in (3, 1, 2):
         wait_recv(result(lax.rem(x + ra, SIDE)), osend.at[0], orecv.at[ra])
-    drain()
+    drain(len(sent))
 
 
 def on_device(tokens, w_query, w_key, w_value, w_out, q_gain, k_gain, key_tiles, key_count):

time: 122 us -> 120 us (0.984)
  Pallas kernels: 120 us -> 118 us
    pallas_call x1, Pallas kernels: 120 us -> 118 us  [on_device(): pl.pallas_call(block_kernel, out_shape=jax.ShapeDtypeStruct((192, SLOTS),...]
where the time goes in v6:
time: 120 us
  Pallas kernels  118 us (98%)
  local copies, waits for them, and re-layouts  1.92 us (2%)
    pallas_call x1, Pallas kernels, on_device(): pl.pallas_call(block_kernel, out_shape=jax.ShapeDtypeStruct((192, SLOTS),...  118 us

profile of v6, /device:TPU:2, one launch (start us, length us, event | category | flops | bytes accessed | tf_op | source)
XLA Modules:
  0.0 119.6 jit_solution(17274737868425370840)
XLA Ops:
  0.0 117.7 %block_attention.1 = bf16[192,1536]{1,0:T(8,128)(2,1)} custom-call(s32[8,24]{1,0:T(8,128)} %bitcast.5, s32[24]{0:T(128)} %count_hbm.1, bf16[96,3072]{1,0:T(8,128)(2,1)} %tok_ref.1, bf16[192,192]{1,0:T(8,128)(2,1)} %wq_ref.1, bf16[192,192]{1,0:T(8,128)(2,1)} %wk_ref.1, bf16[192,192]{1,0:T(8,128)(2,1)} %wv_ref.1, bf16[192,192]{1,0:T(8,128)(2,1)} %wo_ref.1, ...), custom_call_target="tpu_custom_call" | custom-call | tf_op jit(solution)/shard_map/block_attention/pallas_call | solution.py:511
  117.7 1.9 %copy.11 = bf16[1536,192]{0,1:T(8,128)(2,1)} copy(bf16[1536,192]{0,1:T(8,128)(2,1)} %bitcast.4) | data formatting | bytes 1179648
